TPU v7x, 32 devices: a whole 2x2x4 slice. The times are simulated.
32 devices in a mesh: chan: 8 (over y, x, core), tm: 4 (over z).
Axes of the slice: x: 2, y: 2, z: 4, core: 2. Of those that a mesh axis runs over, the one named last changes fastest.
Arguments:
- samples: bfloat16 [256, 96, 4096], P('chan', 'tm'), may hold values from -6 to 6
- taps: float32 [16, 4096], replicated, may hold values from -1.5 to 1.5
- block_tile: int32 [120], replicated, may hold values from 0 to 7, as said below
- tile_slots: int32 [8], replicated, may hold values from 0 to 7, as said below
- kern_u: bfloat16 [16, 30720], replicated, may hold values from -1.1953125 to 1.1953125
- kern_v: bfloat16 [16, 30720], replicated, may hold values from -1.1953125 to 1.1953125
Outputs:
- uv_grid: float32 [8, 2048, 2, 256], P('tm', 'chan')
Inputs may be any that keep to these rules, and one draw needn't show every extreme that they name: `block_tile`: A tile's owner is (its position in tile_slots) // 2. The blocks that fall in the tiles of one owner are at most 60; in every draw one owner has exactly 60. `tile_slots`: each tile number stands once.
All inputs are finite; a program needn't handle non-finite values.
Results may differ from a plain program's by a relative error of at most 0.0077.
Values may be sent and summed in bfloat16 or wider, within the bound.
A program may use at most 192 MiB of HBM per device.

v0:
```python
import math

import jax
import jax.numpy as jnp
import numpy as np
from jax import lax
from jax.sharding import PartitionSpec as P

SBLK = 16
GRID = 16


def passed_along(value, axis, steps):
    count = lax.axis_size(axis)
    leading, last = (max(0, -steps), min(count, count - steps))
    return lax.ppermute(value, axis, [(source, source + steps) for source in range(leading, last)])


def block_pairs(block_total):
    left_list = []
    right_list = []
    for p in range(block_total):
        for q in range(p + 1, block_total):
            left_list.append(p)
            right_list.append(q)
    return (np.array(left_list, dtype=np.int32), np.array(right_list, dtype=np.int32))


def make_kernel(u_part, v_part, block_total):
    u_cols = u_part.astype(jnp.float32).reshape(GRID, block_total, SBLK * SBLK).transpose(1, 2, 0)
    v_cols = v_part.astype(jnp.float32).reshape(GRID, block_total, SBLK * SBLK).transpose(1, 2, 0)
    product = u_cols[:, :, :, None] * v_cols[:, :, None, :]
    return product.reshape(block_total, SBLK * SBLK, GRID * GRID).astype(jnp.bfloat16)


def body(samples, taps, block_tile, tile_slots, kern_u, kern_v):
    station_count, frame_count, length = samples.shape
    channel_count = length // 2
    chan_size = lax.axis_size("chan")
    tm_size = lax.axis_size("tm")
    group_count = chan_size * tm_size
    group_width = channel_count // group_count
    tap_count = taps.shape[0]
    history = passed_along(samples[:, frame_count - (tap_count - 1) :], "tm", 1)
    padded = jnp.concatenate([history, samples], axis=1)
    filtered = jnp.zeros((station_count, frame_count, length), jnp.float32)
    for tap_index in range(tap_count):
        offset = tap_count - 1 - tap_index
        filtered = filtered + taps[tap_index] * padded[:, offset : offset + frame_count].astype(
            jnp.float32
        )
    rows_in = filtered.astype(jnp.bfloat16).reshape(station_count * frame_count, length)
    dft_scale = 1.0 / math.sqrt(length)
    block_cols = min(channel_count, 256)
    groups_per_block = block_cols // group_width
    positions = jnp.arange(length, dtype=jnp.int32)[:, None, None]
    pieces = []
    for column_block in range(channel_count // block_cols):
        channels = column_block * block_cols + jnp.arange(block_cols, dtype=jnp.int32).reshape(
            1, groups_per_block, group_width
        )
        phase_int = positions * channels % length
        phase_angle = phase_int.astype(jnp.float32) * (2.0 * math.pi / length)
        cosine = jnp.cos(phase_angle).astype(jnp.bfloat16)
        sine_neg = (-jnp.sin(phase_angle)).astype(jnp.bfloat16)
        dft_table = jnp.stack([cosine, sine_neg], axis=2).reshape(length, 2 * block_cols)
        spectrum = (
            lax.dot_general(
                dft_table, rows_in, (((0,), (1,)), ((), ())), preferred_element_type=jnp.float32
            )
            * dft_scale
        )
        pieces.append(
            spectrum.astype(jnp.bfloat16).reshape(
                groups_per_block, 2, group_width, station_count, frame_count
            )
        )
    spectra = jnp.concatenate(pieces, axis=0)
    stations = station_count * chan_size
    frames = frame_count * tm_size
    arranged = spectra.reshape(chan_size, tm_size, 2, group_width, station_count, frame_count)
    turned = lax.all_to_all(
        lax.all_to_all(arranged, "chan", split_axis=0, concat_axis=4, tiled=True),
        "tm",
        split_axis=1,
        concat_axis=5,
        tiled=True,
    )
    turned = turned.reshape(2, group_width, stations, frames)
    block_rows = stations // SBLK
    block_total = block_rows * (block_rows - 1) // 2
    vis_scale = 1.0 / math.sqrt(frames)
    swapped = jnp.stack([turned[1], -turned[0]], axis=0)
    real_part = (
        jnp.einsum("cgib,cgjb->gij", turned, turned, preferred_element_type=jnp.float32) * vis_scale
    )
    imag_part = (
        jnp.einsum("cgib,cgjb->gij", swapped, turned, preferred_element_type=jnp.float32)
        * vis_scale
    )
    left_idx, right_idx = block_pairs(block_rows)
    visibility = jnp.stack([real_part, imag_part], axis=1).reshape(
        group_width, 2, block_rows, SBLK, block_rows, SBLK
    )
    visibility = visibility[:, :, left_idx, :, right_idx, :]
    blocks = visibility.reshape(block_total, group_width, 2, SBLK * SBLK).astype(jnp.bfloat16)
    tile_count = tile_slots.shape[0]
    slot_ids = jnp.arange(tile_count, dtype=jnp.int32)
    tile_match = block_tile[:, None] == tile_slots[None, :]
    slot_of_block = jnp.sum(jnp.where(tile_match, slot_ids[None, :], 0), axis=1)
    kernel = make_kernel(kern_u, kern_v, block_total)
    per_block = jnp.einsum("mgce,mel->mgcl", blocks, kernel, preferred_element_type=jnp.float32)
    slot_hits = (slot_of_block[:, None] == slot_ids[None, :]).astype(jnp.float32)
    partial_value = jnp.einsum(
        "mgcl,ms->sgcl", per_block, slot_hits, precision=lax.Precision.HIGHEST
    )
    uv_grid = lax.all_to_all(partial_value, "tm", split_axis=0, concat_axis=1, tiled=True)
    return uv_grid


def solution(mesh):
    placed = (P("chan", "tm", None), P(), P(), P(), P(), P())
    return jax.shard_map(
        body, mesh=mesh, in_specs=placed, out_specs=P("tm", "chan", None, None), check_vma=False
    )
```

profile of v0, /device:TPU:0, one launch (start us, length us, event | category | flops | bytes accessed | tf_op | source)
XLA Modules:
  0.0 871.3 jit_solution(201624281211155769)
XLA Ops:
  12.9 18.1 %cosine_convert_fusion.7 = (bf16[4096,4,1,64]{0,3,2,1:T(8,128)(2,1)S(1)}, bf16[4096,4,1,64]{0,3,2,1:T(8,128)(2,1)S(1)}) fusion(s32[4,64]{1,0:T(4,128)S(1)} %multiply_add_fusion), kind=kLoop, calls=%fused_computation.139 | loop fusion | flops 17825792 | bytes 4195328 | tf_op jit(solution)/shard_map/convert_element_type | solution.py:64
  31.0 18.1 %cosine_convert_fusion.6 = (bf16[4096,4,1,64]{0,3,2,1:T(8,128)(2,1)S(1)}, bf16[4096,4,1,64]{0,3,2,1:T(8,128)(2,1)S(1)}) fusion(s32[4,64]{1,0:T(4,128)S(1)} %fusion.75), kind=kLoop, calls=%fused_computation.135 | loop fusion | flops 17825792 | bytes 4195328 | tf_op jit(solution)/shard_map/convert_element_type | solution.py:64
  49.2 18.1 %cosine_convert_fusion.5 = (bf16[4096,4,1,64]{0,3,2,1:T(8,128)(2,1)S(1)}, bf16[4096,4,1,64]{0,3,2,1:T(8,128)(2,1)S(1)}) fusion(s32[4,64]{1,0:T(4,128)S(1)} %fusion.74), kind=kLoop, calls=%fused_computation.131 | loop fusion | flops 17825792 | bytes 4195328 | tf_op jit(solution)/shard_map/convert_element_type | solution.py:64
  67.3 18.1 %cosine_convert_fusion.4 = (bf16[4096,4,1,64]{0,3,2,1:T(8,128)(2,1)S(1)}, bf16[4096,4,1,64]{0,3,2,1:T(8,128)(2,1)S(1)}) fusion(s32[4,64]{1,0:T(4,128)S(1)} %fusion.73), kind=kLoop, calls=%fused_computation.127 | loop fusion | flops 17825792 | bytes 4195328 | tf_op jit(solution)/shard_map/convert_element_type | solution.py:64
  85.4 18.1 %cosine_convert_fusion.3 = (bf16[4096,4,1,64]{0,3,2,1:T(8,128)(2,1)S(1)}, bf16[4096,4,1,64]{0,3,2,1:T(8,128)(2,1)S(1)}) fusion(s32[4,64]{1,0:T(4,128)S(1)} %fusion.72), kind=kLoop, calls=%fused_computation.123 | loop fusion | flops 17825792 | bytes 4195328 | tf_op jit(solution)/shard_map/convert_element_type | solution.py:64
  103.5 18.1 %cosine_convert_fusion.2 = (bf16[4096,4,1,64]{0,3,2,1:T(8,128)(2,1)S(1)}, bf16[4096,4,1,64]{0,3,2,1:T(8,128)(2,1)S(1)}) fusion(s32[4,64]{1,0:T(4,128)S(1)} %fusion.71), kind=kLoop, calls=%fused_computation.119 | loop fusion | flops 17825792 | bytes 4195328 | tf_op jit(solution)/shard_map/convert_element_type | solution.py:64
  135.9 18.0 %cosine_convert_fusion.1 = (bf16[4096,4,1,64]{0,3,2,1:T(8,128)(2,1)S(1)}, bf16[4096,4,1,64]{0,3,2,1:T(8,128)(2,1)S(1)}) fusion(s32[4,64]{1,0:T(4,128)S(1)} %fusion.70), kind=kLoop, calls=%fused_computation.115 | loop fusion | flops 17825792 | bytes 4195328 | tf_op jit(solution)/shard_map/convert_element_type | solution.py:64
  156.3 18.2 %cosine_convert_fusion = (bf16[4096,4,1,64]{0,3,2,1:T(8,128)(2,1)S(1)}, bf16[4096,4,1,64]{0,3,2,1:T(8,128)(2,1)S(1)}) fusion(s32[4,64]{1,0:T(4,128)S(1)} %fusion.69), kind=kLoop, calls=%fused_computation.111 | loop fusion | flops 17825792 | bytes 4195328 | tf_op jit(solution)/shard_map/convert_element_type | solution.py:64
  183.5 69.1 %add_convert_fusion = bf16[32,24,4096]{2,1,0:T(8,128)(2,1)} fusion(bf16[32,24,4096]{2,1,0:T(8,128)(2,1)} %param.10, bf16[32,15,4096]{2,1,0:T(8,128)(2,1)} %copy.86, f32[4096]{0:T(1024)S(1)} %bitcast.156, f32[4096]{0:T(1024)S(1)} %bitcast.157, f32[4096]{0:T(1024)S(1)} %bitcast.143, f32[4096]{0:T(1024)S(1)} %bitcast.144, f32[4096]{0:T(1024)S(1)} %bitcast.145, ...), kind=kLoop, calls=%fused_computation.35 | loop fusion | flops 292552704 | bytes 16777216 | tf_op jit(solution)/shard_map/convert_element_type | solution.py:52
  379.0 13.6 %copy.125 = bf16[8,4,2,64,32,24]{3,5,4,2,1,0:T(8,128)(2,1)} copy(bf16[8,4,2,64,32,24]{3,2,1,0,5,4:T(2,128)(2,1)} %bitcast.120) | data formatting | bytes 12582912 | tf_op jit(solution)/shard_map/reshape | solution.py:81
  392.5 13.7 %reshape.779 = bf16[8,2,196608]{2,1,0:T(2,128)(2,1)} reshape(bf16[8,4,2,32,24,64]{5,4,3,2,1,0:T(8,128)(2,1)} %bitcast.117) | data formatting | bytes 12582912
  406.3 76.9 %all_to_all.51 = bf16[8,2,196608]{2,1,0:T(2,128)(2,1)} all-to-all(bf16[8,2,196608]{2,1,0:T(2,128)(2,1)} %reshape.779), channel_id=1, replica_groups=mesh['chan'=8,'tm'=4] {'chan'}, dimensions={0} | all-to-all | bytes 12582912 | tf_op jit(solution)/shard_map/all_to_all | solution.py:83
  483.2 13.3 %reshape.780 = bf16[8,4,2,32,24,64]{5,4,3,2,1,0:T(8,128)(2,1)} reshape(bf16[8,2,196608]{2,1,0:T(2,128)(2,1)} %all_to_all.51) | data formatting | bytes 12582912
  509.6 15.4 %copy.97 = bf16[1,4,2,64,256,24]{4,5,3,2,0,1:T(8,128)(2,1)} copy(bf16[1,4,2,64,256,24]{3,5,4,2,1,0:T(8,128)(2,1)} %bitcast.118) | data formatting | bytes 12582912 | tf_op jit(solution)/shard_map/all_to_all | solution.py:83
  540.8 127.7 %all-to-all-done.1 = bf16[1,4,2,64,256,24]{4,5,3,2,0,1:T(8,128)(2,1)} async-done(((bf16[1,4,2,64,256,24]{4,5,3,2,0,1:T(8,128)(2,1)}), bf16[1,4,2,64,256,24]{4,5,3,2,0,1:T(8,128)(2,1)}, u32[]{:S(2)}, u32[]{:S(2)}) %all-to-all-start.1) | async-done | bytes 6291488 | tf_op jit(solution)/shard_map/all_to_all | solution.py:82
  700.8 17.4 %copy.102 = bf16[64,256,256]{0,2,1:T(8,128)(2,1)} copy(bf16[64,256,256]{2,1,0:T(8,128)(2,1)} %bitcast_multiply_fusion) | data formatting | bytes 16777216 | tf_op jit(solution)/shard_map/mul | solution.py:98
  718.2 17.4 %copy.99 = bf16[64,256,256]{0,2,1:T(8,128)(2,1)} copy(bf16[64,256,256]{2,1,0:T(8,128)(2,1)} %bitcast_multiply_fusion.1) | data formatting | bytes 16777216 | tf_op jit(solution)/shard_map/mul | solution.py:95
  735.6 22.7 %pad_maximum_fusion = bf16[64,2,16,16,16,16]{0,5,4,3,2,1:T(8,128)(2,1)} fusion(bf16[64,1,16,16,16,16]{0,5,4,3,2,1:T(8,128)(2,1)} %bitcast.113, bf16[64,1,16,16,16,16]{0,5,4,3,2,1:T(8,128)(2,1)} %bitcast.114), kind=kLoop, calls=%fused_computation.1 | loop fusion | flops 8388608 | bytes 33554432 | tf_op jit(solution)/shard_map/stack | solution.py:102
  758.3 12.2 %gather_fusion = bf16[120,64,2,16,16]{1,4,3,2,0:T(8,128)(2,1)} fusion(bf16[64,2,16,16,16,16]{0,5,4,3,2,1:T(8,128)(2,1)} %pad_maximum_fusion, s32[120]{0:T(128)S(1)} %copy-done), kind=kCustom, calls=%fused_computation | custom fusion | bytes 15729600 | tf_op jit(solution)/shard_map/gather | solution.py:105
  770.5 26.6 %copy.103 = bf16[120,64,2,16,16]{0,4,3,2,1:T(8,128)(2,1)} copy(bf16[120,64,2,16,16]{1,4,3,2,0:T(8,128)(2,1)} %gather_fusion) | data formatting | bytes 15728640 | tf_op jit(solution)/shard_map/gather | solution.py:105
  797.2 12.0 %copy.106 = bf16[120,64,2,256]{3,1,2,0:T(8,128)(2,1)} copy(bf16[120,64,2,256]{0,3,2,1:T(8,128)(2,1)} %bitcast.119) | data formatting | bytes 15728640 | tf_op jit(solution)/shard_map/convert_element_type | solution.py:106
  809.2 13.6 %fusion.80 = f32[120,64,2,256]{3,1,2,0:T(8,128)} fusion(bf16[120,64,2,256]{3,1,2,0:T(8,128)(2,1)} %copy.106, bf16[120,256,256,1]{1,2,3,0:T(8,128)(2,1)} %bitcast.112), kind=kOutput, calls=%fused_computation.186 | convolution fusion | flops 2013265920 | bytes 39321600 | tf_op jit(solution)/shard_map/mgce,mel->mgcl/dot_general | solution.py:112
  822.8 18.7 %fusion = f32[8,64,2,256]{3,0,2,1:T(8,128)S(1)} fusion(f32[120,64,2,256]{3,1,2,0:T(8,128)} %fusion.80, s32[120]{0:T(128)S(1)} %select_reduce_fusion), kind=kOutput, calls=%fused_computation.33 | convolution fusion | flops 377488320 | bytes 16777696 | tf_op jit(solution)/shard_map/mgcl,ms->sgcl/dot_general | solution.py:114
  842.1 27.7 %all_to_all.52 = f32[8,64,2,256]{3,2,1,0:T(2,128)S(1)} all-to-all(f32[8,64,2,256]{3,2,1,0:T(2,128)S(1)} %copy.109), channel_id=1, replica_groups=mesh['chan'=8,'tm'=4] {'tm'}, dimensions={0} | all-to-all | bytes 2097152 | tf_op jit(solution)/shard_map/all_to_all | solution.py:117
  (92 shorter events, 227.6 us)
Async XLA Ops:
  5.8 171.4 %collective-permute-start = (bf16[32,15,4096]{2,0,1:T(8,128)(2,1)S(1)}, bf16[32,15,4096]{2,0,1:T(8,128)(2,1)}, u32[]{:S(2)}, u32[]{:S(2)}) collective-permute-start(bf16[32,15,4096]{2,0,1:T(8,128)(2,1)S(1)} %copy.117), channel_id=1, source_target_pairs={{0,1},{1,2},{2,3},{4,5},{5,6},{6,7},{8,9},{9,10},{10,11},{12,13},{... | collective-permute-start | bytes 11796488 | tf_op jit(solution)/shard_map/ppermute | solution.py:16
  174.6 2.4 copy-start.8
  360.5 5.4 copy-start.1
  360.5 8.0 copy-start.2
  363.2 7.9 copy-start.3
  365.9 7.9 copy-start.4
  368.5 7.9 copy-start.5
  525.0 5.8 copy-start.6
  525.0 6.0 copy-start.7
  525.0 143.6 %all-to-all-start.1 = ((bf16[1,4,2,64,256,24]{4,5,3,2,0,1:T(8,128)(2,1)}), bf16[1,4,2,64,256,24]{4,5,3,2,0,1:T(8,128)(2,1)}, u32[]{:S(2)}, u32[]{:S(2)}) async-start(bf16[1,4,2,64,256,24]{4,5,3,2,0,1:T(8,128)(2,1)} %copy.97), calls=%async_computation.1 | async-start | bytes 12582912 | tf_op jit(solution)/shard_map/all_to_all | solution.py:82
  530.8 0.7 copy-start.9
  530.8 0.7 copy-start.10
  735.6 22.7 %copy-start = (s32[120]{0:T(128)S(1)}, s32[120]{0:T(128)}, u32[]{:S(2)}) copy-start(s32[120]{0:T(128)} %constant.107) | copy-start | bytes 1444
where the time goes:
time: 877 us; the launch traced here: 871 us
  other arithmetic  268 us (31%)
  local copies, waits for them, and re-layouts  241 us (27%)
  waiting for transfers between devices  128 us (15%)
  matrix products  117 us (13%)
  blocking collectives  105 us (12%)
  starting transfers between devices  12.8 us (1%)
    convert_element_type x8, other arithmetic, body(): cosine = jnp.cos(phase_angle).astype(jnp.bfloat16)  145 us
    all_to_all x1, waiting for transfers between devices, body(): lax.all_to_all(lax.all_to_all(arranged, 'chan', split_axis=0, concat_axis...  128 us
    all_to_all x1, blocking collectives, body(): lax.all_to_all(arranged, 'chan', split_axis=0, concat_axis=4, tiled=True)  76.9 us
    convert_element_type x1, other arithmetic, body(): filtered.astype(jnp.bfloat16).reshape(station_count * frame_count, length)  69.1 us
    dot_general x8, matrix products, body(): lax.dot_general(dft_table, rows_in, (((0,), (1,)), ((), ())), preferred_e...  64.6 us
    unnamed x32, local copies, waits for them, and re-layouts  48.3 us
    gather x2, local copies, waits for them, and re-layouts, body(): visibility = visibility[:, :, left_idx, :, right_idx, :]  38.9 us
    all_to_all x3, local copies, waits for them, and re-layouts, body(): lax.all_to_all(arranged, 'chan', split_axis=0, concat_axis=4, tiled=True)  28.5 us
  transfers between devices with their start and end apart: 2, of which 1 were waited for; matrix products, arithmetic and copies ran while one was open for 20% of the time, Pallas kernels for 0%

commit v1 on v0

v1 whole, which is shorter than its diff:
```python
import functools
import math

import jax
import jax.numpy as jnp
import numpy as np
from jax import lax
from jax.experimental import pallas as pl
from jax.experimental.pallas import tpu as pltpu
from jax.sharding import PartitionSpec as P

SBLK = 16
GRID = 16
LANES = 128
HISTORY = 16
VMEM_LIMIT = 60 * 1024 * 1024


def passed_along(value, axis, steps):
    count = lax.axis_size(axis)
    leading, last = (max(0, -steps), min(count, count - steps))
    return lax.ppermute(value, axis, [(source, source + steps) for source in range(leading, last)])


def block_pairs(block_total):
    pairs = [(p, q) for p in range(block_total) for q in range(p + 1, block_total)]
    return np.array(pairs, dtype=np.int32)


def dft_tables(length, chan_size):
    half = length // 2
    channels = length // 2
    width = channels // chan_size // 2
    positions = np.arange(half, dtype=np.int64)[:, None, None]
    tables = []
    for parity in range(2):
        chans = (
            np.arange(chan_size, dtype=np.int64)[:, None] * 2 * width
            + 2 * np.arange(width, dtype=np.int64)[None, :]
            + parity
        )[None]
        angle = ((positions * chans) % length).astype(np.float64) * (2.0 * math.pi / length)
        table = np.stack([np.cos(angle), -np.sin(angle)], axis=2)
        tables.append(table.reshape(half, 2 * channels // 2).astype(jnp.bfloat16))
    return tables


def filter_kernel(lo_ref, hi_ref, hist_lo_ref, hist_hi_ref, taps_lo_ref, taps_hi_ref,
                  even_ref, odd_ref, wide):
    stations, frames, cols = lo_ref.shape
    tap_count = taps_lo_ref.shape[0]
    for side, (hist, body_ref) in enumerate(((hist_lo_ref, lo_ref), (hist_hi_ref, hi_ref))):
        wide[side, :HISTORY] = jnp.swapaxes(hist[...].astype(jnp.float32), 0, 1)
        wide[side, HISTORY:] = jnp.swapaxes(body_ref[...].astype(jnp.float32), 0, 1)
    span = 4
    rows = 16
    for lane in range(0, cols, LANES):
        lanes = slice(lane, lane + LANES)

        def step(index, carry):
            station = pl.multiple_of((index % (stations // rows)) * rows, rows)
            frame = (index // (stations // rows)) * span
            sums = []
            for side, taps_ref in enumerate((taps_lo_ref, taps_hi_ref)):
                values = [
                    wide[side, frame + HISTORY - (tap_count - 1) + k, pl.ds(station, rows), lanes]
                    for k in range(span + tap_count - 1)
                ]
                accs = [jnp.zeros((rows, LANES), jnp.float32) for _ in range(span)]
                for tap in range(tap_count):
                    weight = taps_ref[tap : tap + 1, lanes]
                    for b in range(span):
                        accs[b] = accs[b] + weight * values[b + tap_count - 1 - tap]
                sums.append(accs)
            for b in range(span):
                even_ref[frame + b, pl.ds(station, rows), lanes] = (
                    sums[0][b] + sums[1][b]
                ).astype(jnp.bfloat16)
                odd_ref[frame + b, pl.ds(station, rows), lanes] = (
                    sums[0][b] - sums[1][b]
                ).astype(jnp.bfloat16)
            return carry

        lax.fori_loop(0, (stations // rows) * (frames // span), step, 0)


def filtered_halves(samples, history, taps):
    stations, frames, length = samples.shape
    tap_count = taps.shape[0]
    half = length // 2
    cols = 256
    steps = half // cols
    lo = lambda j: (0, 0, j)
    hi = lambda j: (0, 0, j + steps)
    out = jax.ShapeDtypeStruct((frames, stations, half), jnp.bfloat16)
    out_spec = pl.BlockSpec((frames, stations, cols), lo)
    return pl.pallas_call(
        filter_kernel,
        grid=(steps,),
        in_specs=[
            pl.BlockSpec((stations, frames, cols), lo),
            pl.BlockSpec((stations, frames, cols), hi),
            pl.BlockSpec((stations, HISTORY, cols), lo),
            pl.BlockSpec((stations, HISTORY, cols), hi),
            pl.BlockSpec((tap_count, cols), lambda j: (0, j)),
            pl.BlockSpec((tap_count, cols), lambda j: (0, j + steps)),
        ],
        out_specs=[out_spec, out_spec],
        out_shape=[out, out],
        scratch_shapes=[pltpu.VMEM((2, HISTORY + frames, stations, cols), jnp.float32)],
        compiler_params=pltpu.CompilerParams(vmem_limit_bytes=VMEM_LIMIT),
        cost_estimate=pl.CostEstimate(
            flops=2 * tap_count * samples.size, bytes_accessed=5 * samples.size, transcendentals=0
        ),
    )(samples, samples, history, history, taps, taps)


def dft_kernel(scale, rows_ref, table_ref, out_ref):
    out_ref[0] = (
        jnp.dot(rows_ref[...], table_ref[...], preferred_element_type=jnp.float32) * scale
    ).astype(jnp.bfloat16)


def dft(rows, table, chan_size, scale):
    row_count, depth = rows.shape
    width = table.shape[1] // chan_size
    return pl.pallas_call(
        functools.partial(dft_kernel, scale),
        grid=(chan_size,),
        in_specs=[
            pl.BlockSpec((row_count, depth), lambda c: (0, 0)),
            pl.BlockSpec((depth, width), lambda c: (0, c)),
        ],
        out_specs=pl.BlockSpec((1, row_count, width), lambda c: (c, 0, 0)),
        out_shape=jax.ShapeDtypeStruct((chan_size, row_count, width), jnp.bfloat16),
        compiler_params=pltpu.CompilerParams(vmem_limit_bytes=VMEM_LIMIT),
        cost_estimate=pl.CostEstimate(
            flops=2 * rows.size * table.shape[1],
            bytes_accessed=2 * (rows.size + table.size + row_count * table.shape[1]),
            transcendentals=0,
        ),
    )(rows, table)


def weights_kernel(shift_ref, u_ref, v_ref, out_ref):
    per_step, rows, cells = out_ref.shape
    first = pl.program_id(0) * per_step
    u_of = lax.broadcasted_iota(jnp.int32, (GRID, cells), 1) // GRID
    v_of = lax.broadcasted_iota(jnp.int32, (GRID, cells), 1) % GRID
    grid_row = lax.broadcasted_iota(jnp.int32, (GRID, cells), 0)
    spread_u = (u_of == grid_row).astype(jnp.bfloat16)
    spread_v = (v_of == grid_row).astype(jnp.bfloat16)
    dims = (((0,), (0,)), ((), ()))
    for k in range(per_step):
        shift = shift_ref[first + k]
        for part in range(rows // LANES):
            where = pl.ds(k * rows + part * LANES, LANES)
            u_part = pltpu.roll(u_ref[:, where].astype(jnp.float32), shift, 1).astype(jnp.bfloat16)
            v_part = pltpu.roll(v_ref[:, where].astype(jnp.float32), shift, 1).astype(jnp.bfloat16)
            u_wide = lax.dot_general(u_part, spread_u, dims, preferred_element_type=jnp.float32)
            v_wide = lax.dot_general(v_part, spread_v, dims, preferred_element_type=jnp.float32)
            out_ref[k, part * LANES : (part + 1) * LANES, :] = (u_wide * v_wide).astype(
                jnp.bfloat16
            )


def grid_weights(kern_u, kern_v, shifts):
    rows = SBLK * SBLK
    blocks = kern_u.shape[1] // rows
    per_step = 8
    spec = pl.BlockSpec((GRID, per_step * rows), lambda m, shift: (0, m))
    return pl.pallas_call(
        weights_kernel,
        grid_spec=pltpu.PrefetchScalarGridSpec(
            num_scalar_prefetch=1,
            grid=(blocks // per_step,),
            in_specs=[spec, spec],
            out_specs=pl.BlockSpec((per_step, rows, GRID * GRID), lambda m, shift: (m, 0, 0)),
        ),
        out_shape=jax.ShapeDtypeStruct((blocks, rows, GRID * GRID), jnp.bfloat16),
        compiler_params=pltpu.CompilerParams(vmem_limit_bytes=VMEM_LIMIT),
    )(shifts, kern_u, kern_v)


def correlate_kernel(scale, slot_ref, turned_ref, weights_ref, out_ref, spectra, vis, blocks):
    sources, frames, source_stations, width = turned_ref.shape
    stations = sources * source_stations
    group = width // 2
    tiles, chunks, rows, cells = out_ref.shape
    per_chunk = rows // 2
    half = stations // 2
    half_blocks = half // SBLK
    block_rows = stations // SBLK
    pieces = LANES // SBLK

    out_ref[...] = jnp.zeros_like(out_ref)

    def turn(frame, carry):
        values = turned_ref[:, frame].astype(jnp.float32).reshape(stations, width)
        flipped = values.T
        where = pl.ds(pl.multiple_of(frame * width, width), width)
        for side in range(2):
            spectra[side, where, :] = flipped[:, side * LANES : (side + 1) * LANES]
        return carry

    lax.fori_loop(0, frames, turn, 0)

    lane_piece = lax.broadcasted_iota(jnp.int32, (16, LANES), 1) // SBLK
    masks = [(lane_piece & (1 << bit)) != 0 for bit in range(3)]

    def chunk_step(chunk, carry):
        for phase in range(2):
            sides = (0, 1) if phase == 0 else (1,)

            def channel(index, inner):
                channel_index = chunk * per_chunk + index
                real = [
                    spectra.at[s][pl.ds(channel_index, frames, stride=width), :] for s in range(2)
                ]
                imag = [
                    spectra.at[s][pl.ds(group + channel_index, frames, stride=width), :]
                    for s in range(2)
                ]
                right = jnp.concatenate(
                    [jnp.concatenate([real[s], imag[s]], axis=0) for s in sides], axis=1
                ).astype(jnp.bfloat16)
                left = jnp.concatenate(
                    [
                        jnp.concatenate([real[phase], imag[phase]], axis=0),
                        jnp.concatenate([imag[phase], -real[phase]], axis=0),
                    ],
                    axis=1,
                ).astype(jnp.bfloat16)
                product = (
                    lax.dot_general(
                        left, right, (((0,), (0,)), ((), ())), preferred_element_type=jnp.float32
                    )
                    * scale
                )
                for part in range(2):
                    for place, side in enumerate(sides):
                        vis.at[side][pl.ds(part * per_chunk + index, half, stride=rows), :] = (
                            product[
                                part * half : (part + 1) * half,
                                place * LANES : (place + 1) * LANES,
                            ]
                        )
                return inner

            lax.fori_loop(0, per_chunk, channel, 0)

            def block_row(local, inner):
                p = phase * half_blocks + local
                for side in sides:
                    def rearrange(tile, innermost):
                        row = pl.multiple_of(tile * 16, 16)
                        for upper in range(2):
                            turned = []
                            for a in range(pieces):
                                start = pl.multiple_of(
                                    (local * SBLK + upper * pieces + a) * rows, rows
                                )
                                value = vis[side, pl.ds(start + row, 16), :]
                                if a:
                                    value = pltpu.roll(value, a * SBLK, 1)
                                turned.append(value)
                            for bit in range(3):
                                turned = [
                                    jnp.where(
                                        masks[bit], turned[(x + (1 << bit)) % pieces], turned[x]
                                    )
                                    for x in range(pieces)
                                ]
                            for piece in range(pieces):
                                blocks[
                                    piece,
                                    pl.ds(row, 16),
                                    upper * LANES : (upper + 1) * LANES,
                                ] = turned[-piece % pieces].astype(jnp.bfloat16)
                        return innermost

                    lax.fori_loop(0, rows // 16, rearrange, 0)
                    for piece in range(pieces):
                        q = side * pieces + piece

                        @pl.when(q > p)
                        def _():
                            m = p * (2 * block_rows - p - 1) // 2 + q - p - 1
                            slot = slot_ref[m]
                            out_ref[slot, chunk] += jnp.dot(
                                blocks[piece],
                                weights_ref[m],
                                preferred_element_type=jnp.float32,
                            )
                return inner

            lax.fori_loop(0, half_blocks, block_row, 0)
        return carry

    lax.fori_loop(0, chunks, chunk_step, 0)


def gridded(turned, weights, slot_of_block, tile_count, total_frames):
    sources, frames, source_stations, width = turned.shape
    stations = sources * source_stations
    group = width // 2
    per_chunk = min(group, 64)
    chunks = group // per_chunk
    rows = 2 * per_chunk
    cells = GRID * GRID
    whole = pl.BlockSpec(memory_space=pltpu.VMEM)
    return pl.pallas_call(
        functools.partial(correlate_kernel, 1.0 / math.sqrt(total_frames)),
        in_specs=[pl.BlockSpec(memory_space=pltpu.SMEM), whole, whole],
        out_specs=whole,
        out_shape=jax.ShapeDtypeStruct((tile_count, chunks, rows, cells), jnp.float32),
        scratch_shapes=[
            pltpu.VMEM((2, frames * width, LANES), jnp.float32),
            pltpu.VMEM((2, stations // 2 * rows, LANES), jnp.float32),
            pltpu.VMEM((LANES // SBLK, rows, SBLK * SBLK), jnp.bfloat16),
        ],
        compiler_params=pltpu.CompilerParams(vmem_limit_bytes=VMEM_LIMIT),
        cost_estimate=pl.CostEstimate(
            flops=2 * weights.size * rows * chunks,
            bytes_accessed=2 * (weights.size + turned.size),
            transcendentals=0,
        ),
    )(slot_of_block, turned, weights)


def body(samples, taps, block_tile, tile_slots, kern_u, kern_v):
    station_count, frame_count, length = samples.shape
    chan_size = lax.axis_size("chan")
    tm_size = lax.axis_size("tm")
    half = length // 2
    history = passed_along(samples[:, frame_count - HISTORY :], "tm", 1)
    halves = filtered_halves(samples, history, taps)
    tables = dft_tables(length, chan_size)
    dft_scale = 1.0 / math.sqrt(length)

    tile_count = tile_slots.shape[0]
    slot_ids = jnp.arange(tile_count, dtype=jnp.int32)
    tile_match = block_tile[:, None] == tile_slots[None, :]
    slot_of_block = jnp.sum(jnp.where(tile_match, slot_ids[None, :], 0), axis=1).astype(jnp.int32)
    pairs = block_pairs(station_count * chan_size // SBLK)
    pieces = LANES // SBLK
    shifts = jnp.asarray((pairs[:, 1] % pieces) * SBLK, jnp.int32)
    weights = grid_weights(kern_u, kern_v, shifts)

    grids = []
    for parity in range(2):
        rows_in = halves[parity].reshape(frame_count * station_count, half)
        spectrum = dft(rows_in, jnp.asarray(tables[parity]), chan_size, dft_scale)
        turned = lax.all_to_all(spectrum, "chan", split_axis=0, concat_axis=0, tiled=True)
        turned = turned.reshape(chan_size, frame_count, station_count, spectrum.shape[-1])
        partial_grid = gridded(
            turned, weights, slot_of_block, tile_count, frame_count * tm_size
        )
        owned = lax.psum_scatter(partial_grid, "tm", scatter_dimension=0, tiled=True)
        owned_tiles, chunks, rows, cells = owned.shape
        owned = owned.reshape(owned_tiles, chunks, 2, rows // 2, cells).transpose(0, 1, 3, 2, 4)
        grids.append(owned.reshape(owned_tiles, chunks * rows // 2, 1, 2, cells))
    uv_grid = jnp.concatenate(grids, axis=2)
    return uv_grid.reshape(uv_grid.shape[0], -1, 2, uv_grid.shape[-1])


def solution(mesh):
    placed = (P("chan", "tm", None), P(), P(), P(), P(), P())
    return jax.shard_map(
        body, mesh=mesh, in_specs=placed, out_specs=P("tm", "chan", None, None), check_vma=False
    )
```

time: 877 us -> 683 us (0.78)
  Pallas kernels: 0 us -> 457 us
  other arithmetic: 268 us -> 0.66 us
  local copies, waits for them, and re-layouts: 241 us -> 8.08 us
  matrix products: 117 us -> 0 us
  blocking collectives: 105 us -> 42.3 us
  waiting for transfers between devices: 128 us -> 150 us
  between operations: 0.57 us -> 13.5 us
    pallas_call x0 -> x6, Pallas kernels: none -> 457 us  [the longest x2 386 us: gridded(): pl.pallas_call(functools.partial(correlate_kernel, 1.0 / math.sqrt(total_...]
    convert_element_type x10 -> x0, other arithmetic: 223 us -> none  [the longest x8 145 us: body(): cosine = jnp.cos(phase_angle).astype(jnp.bfloat16)]
    dot_general x12 -> x0, matrix products: 117 us -> none  [the longest x8 64.6 us: body(): lax.dot_general(dft_table, rows_in, (((0,), (1,)), ((), ())), preferred_e...]
    all_to_all x1, waiting for transfers between devices: 128 us -> 18.8 us  [body(): lax.all_to_all(spectrum, 'chan', split_axis=0, concat_axis=0, tiled=True)]
    ppermute x1, waiting for transfers between devices: 0.01 us -> 87.9 us  [passed_along(): lax.ppermute(value, axis, [(source, source + steps) for source in range(l...]
    all_to_all x2 -> x1, blocking collectives: 105 us -> 42.3 us  [body(): lax.all_to_all(spectrum, 'chan', split_axis=0, concat_axis=0, tiled=True)]
    unnamed x32 -> x6, local copies, waits for them, and re-layouts: 48.3 us -> 1.67 us
    reduce_scatter x0 -> x2, waiting for transfers between devices: none -> 43.3 us  [body(): lax.psum_scatter(partial_grid, 'tm', scatter_dimension=0, tiled=True)]
  transfers between devices with their start and end apart: 2 -> 4, of which waited for: 1 -> 3; matrix products, arithmetic and copies ran while one was open for 20% -> 0% of each run, Pallas kernels for 0% -> 33%
where the time goes in v1:
time: 683 us; the launch traced here: 682 us
  Pallas kernels  457 us (67%)
  waiting for transfers between devices  150 us (22%)
  blocking collectives  42.3 us (6%)
  between operations  13.5 us (2%)
  starting transfers between devices  10.7 us (2%)
  local copies, waits for them, and re-layouts  8.08 us (1%)
    pallas_call x2, Pallas kernels, gridded(): pl.pallas_call(functools.partial(correlate_kernel, 1.0 / math.sqrt(total_...  386 us
    ppermute x1, waiting for transfers between devices, passed_along(): lax.ppermute(value, axis, [(source, source + steps) for source in range(l...  87.9 us
    reduce_scatter x2, waiting for transfers between devices, body(): lax.psum_scatter(partial_grid, 'tm', scatter_dimension=0, tiled=True)  43.3 us
    all_to_all x1, blocking collectives, body(): lax.all_to_all(spectrum, 'chan', split_axis=0, concat_axis=0, tiled=True)  42.3 us
    pallas_call x1, Pallas kernels, filtered_halves(): pl.pallas_call(filter_kernel, grid=(steps,), in_specs=[pl.BlockSpec((stat...  27.7 us
    pallas_call x2, Pallas kernels, dft(): pl.pallas_call(functools.partial(dft_kernel, scale), grid=(chan_size,), i...  24.7 us
    all_to_all x1, waiting for transfers between devices, body(): lax.all_to_all(spectrum, 'chan', split_axis=0, concat_axis=0, tiled=True)  18.8 us
    pallas_call x1, Pallas kernels, grid_weights(): pl.pallas_call(weights_kernel, grid_spec=pltpu.PrefetchScalarGridSpec(num...  18.4 us
  transfers between devices with their start and end apart: 4, of which 3 were waited for; matrix products, arithmetic and copies ran while one was open for 0% of the time, Pallas kernels for 33%

profile of v1, /device:TPU:0, one launch (start us, length us, event | category | flops | bytes accessed | tf_op | source)
XLA Modules:
  0.0 681.8 jit_solution(15966652394766069745)
XLA Ops:
  6.5 2.5 slice.3
  9.0 6.9 %collective-permute-start = (bf16[32,16,4096]{2,1,0:T(8,128)(2,1)S(1)}, bf16[32,16,4096]{2,1,0:T(8,128)(2,1)}, u32[]{:S(2)}, u32[]{:S(2)}) collective-permute-start(bf16[32,16,4096]{2,1,0:T(8,128)(2,1)S(1)} %slice.3), channel_id=1, source_target_pairs={{0,1},{1,2},{2,3},{4,5},{5,6},{6,7},{8,9},{9,10},{10,11},{12,13},{... | collective-permute-start | bytes 12582920 | tf_op jit(solution)/shard_map/ppermute | solution.py:22
  15.9 87.9 %collective-permute-done.hist_lo_ref.hist_hi_ref = bf16[32,16,4096]{2,1,0:T(8,128)(2,1)} collective-permute-done((bf16[32,16,4096]{2,1,0:T(8,128)(2,1)S(1)}, bf16[32,16,4096]{2,1,0:T(8,128)(2,1)}, u32[]{:S(2)}, u32[]{:S(2)}) %collective-permute-start) | collective-permute-done | bytes 4194336 | tf_op jit(solution)/shard_map/ppermute | solution.py:22
  103.7 27.7 %shard_map.91 = (bf16[24,32,2048]{2,1,0:T(8,128)(2,1)}, bf16[24,32,2048]{2,1,0:T(8,128)(2,1)}) custom-call(bf16[32,24,4096]{2,1,0:T(8,128)(2,1)} %hi_ref.1, bf16[32,24,4096]{2,1,0:T(8,128)(2,1)} %hi_ref.1, bf16[32,16,4096]{2,1,0:T(8,128)(2,1)} %collective-permute-done.hist_lo_ref.hist_hi_ref, ...), custom_call_target="tpu_custom_call" | custom-call | flops 100663296 | bytes 15728640 | tf_op jit(solution)/shard_map/pallas_call | solution.py:97
  131.4 12.3 %shard_map.92 = bf16[8,768,256]{2,1,0:T(8,128)(2,1)} custom-call(bf16[768,2048]{1,0:T(8,128)(2,1)} %bitcast.20, bf16[2048,2048]{1,0:T(8,128)(2,1)} %constant.9.clone.table_ref), custom_call_target="tpu_custom_call" | custom-call | flops 6442450944 | bytes 14680064 | tf_op jit(solution)/shard_map/pallas_call | solution.py:127
  143.7 3.7 all-to-all-start
  147.5 0.0 reduce-scatter.3.cloned.1.call-start
  147.5 18.4 %shard_map.93.weights_ref = bf16[120,256,256]{2,1,0:T(8,128)(2,1)} custom-call(s32[120]{0:T(128)} %constant.8.clone.shift_ref, bf16[16,30720]{1,0:T(8,128)(2,1)} %u_ref.1, bf16[16,30720]{1,0:T(8,128)(2,1)} %v_ref.1), custom_call_target="tpu_custom_call" | custom-call | tf_op jit(solution)/shard_map/pallas_call | solution.py:172
  166.0 0.6 select_reduce_fusion.slot_ref
  166.6 18.8 %all-to-all-done = bf16[8,768,256]{2,1,0:T(8,128)(2,1)S(1)} async-done(((bf16[8,768,256]{2,1,0:T(8,128)(2,1)}), bf16[8,768,256]{2,1,0:T(8,128)(2,1)S(1)}, u32[]{:S(2)}, u32[]{:S(2)}) %all-to-all-start) | async-done | bytes 3145760 | tf_op jit(solution)/shard_map/all_to_all | solution.py:354
  185.3 1.7 copy-done
  187.0 193.0 %shard_map.94 = f32[8,2,128,256]{3,2,1,0:T(8,128)} custom-call(s32[120]{0:T(128)} %select_reduce_fusion.slot_ref, bf16[8,24,32,256]{3,2,1,0:T(8,128)(2,1)} %bitcast.13, bf16[120,256,256]{2,1,0:T(8,128)(2,1)} %shard_map.93.weights_ref), custom_call_target="tpu_custom_call" | custom-call | flops 4026531840 | bytes 18874368 | tf_op jit(solution)/shard_map/pallas_call | solution.py:312
  380.0 0.0 reduce-scatter.3.cloned.1.call-update
  380.0 0.0 reduce-scatter.5.cloned.1.call-start
  380.1 12.4 %shard_map.95 = bf16[8,768,256]{2,1,0:T(8,128)(2,1)} custom-call(bf16[768,2048]{1,0:T(8,128)(2,1)} %bitcast.19, bf16[2048,2048]{1,0:T(8,128)(2,1)} %constant.10.clone.table_ref), custom_call_target="tpu_custom_call" | custom-call | flops 6442450944 | bytes 14680064 | tf_op jit(solution)/shard_map/pallas_call | solution.py:127
  392.4 42.3 %all_to_all.10 = bf16[8,768,256]{2,1,0:T(8,128)(2,1)} all-to-all(bf16[8,768,256]{2,1,0:T(8,128)(2,1)} %shard_map.95), channel_id=1, replica_groups=mesh['chan'=8,'tm'=4] {'chan'}, dimensions={0} | all-to-all | bytes 6291456 | tf_op jit(solution)/shard_map/all_to_all | solution.py:354
  434.7 192.9 %shard_map.96 = f32[8,2,128,256]{3,2,1,0:T(8,128)} custom-call(s32[120]{0:T(128)} %select_reduce_fusion.slot_ref, bf16[8,24,32,256]{3,2,1,0:T(8,128)(2,1)} %bitcast.14, bf16[120,256,256]{2,1,0:T(8,128)(2,1)} %shard_map.93.weights_ref), custom_call_target="tpu_custom_call" | custom-call | flops 4026531840 | bytes 18874368 | tf_op jit(solution)/shard_map/pallas_call | solution.py:312
  627.6 0.0 reduce-scatter.5.cloned.1.call-update
  627.7 0.0 reduce-scatter.3.cloned.1.call-done
  627.7 1.1 copy.15
  628.8 43.2 %reduce-scatter.5.cloned.1.call-done = f32[2,2,128,256]{3,2,1,0:T(8,128)} async-done(((f32[8,2,128,256]{3,2,1,0:T(8,128)}), f32[2,2,128,256]{3,2,1,0:T(8,128)}) %reduce-scatter.5.cloned.1.call-update) | async-done | bytes 524304 | tf_op jit(solution)/shard_map/reduce_scatter | solution.py:359
  672.0 1.1 copy.16
  673.1 0.1 pad_maximum_fusion
  673.2 1.8 copy.17
  (5 shorter events, 0.0 us)
Async XLA Ops:
  9.0 94.7 %collective-permute-start = (bf16[32,16,4096]{2,1,0:T(8,128)(2,1)S(1)}, bf16[32,16,4096]{2,1,0:T(8,128)(2,1)}, u32[]{:S(2)}, u32[]{:S(2)}) collective-permute-start(bf16[32,16,4096]{2,1,0:T(8,128)(2,1)S(1)} %slice.3), channel_id=1, source_target_pairs={{0,1},{1,2},{2,3},{4,5},{5,6},{6,7},{8,9},{9,10},{10,11},{12,13},{... | collective-permute-start | bytes 12582920 | tf_op jit(solution)/shard_map/ppermute | solution.py:22
  143.7 41.6 %all-to-all-start = ((bf16[8,768,256]{2,1,0:T(8,128)(2,1)}), bf16[8,768,256]{2,1,0:T(8,128)(2,1)S(1)}, u32[]{:S(2)}, u32[]{:S(2)}) async-start(bf16[8,768,256]{2,1,0:T(8,128)(2,1)} %shard_map.92), calls=%async_computation | async-start | bytes 6291456 | tf_op jit(solution)/shard_map/all_to_all | solution.py:354
  147.4 18.5 %copy-start.1 = (s32[120]{0:T(128)S(1)}, s32[120]{0:T(128)}, u32[]{:S(2)}) copy-start(s32[120]{0:T(128)} %param.11) | copy-start | bytes 1444
  147.5 18.5 %copy-start.2 = (s32[8]{0:T(128)S(1)}, s32[8]{0:T(128)}, u32[]{:S(2)}) copy-start(s32[8]{0:T(128)} %param.12) | copy-start | bytes 100
  147.5 480.2 %reduce-scatter.3.cloned.1.call-start = ((), (), s32[]{:S(2)}) async-start(), calls=%async_computation.4 | async-start | bytes 2621440 | tf_op jit(solution)/shard_map/reduce_scatter | solution.py:359
  185.3 1.7 copy-start
  380.0 292.0 %reduce-scatter.5.cloned.1.call-start = ((), (), s32[]{:S(2)}) async-start(), calls=%async_computation.5 | async-start | bytes 2621440 | tf_op jit(solution)/shard_map/reduce_scatter | solution.py:359
Sparse Core Ops, SparseCore 0:
  380.1 44.2 reduce-scatter.2
  627.8 44.1 reduce-scatter.4

commit v2 on v1

v2 whole, which is shorter than its diff:
```python
import functools
import math

import jax
import jax.numpy as jnp
import numpy as np
from jax import lax
from jax.experimental import pallas as pl
from jax.experimental.pallas import tpu as pltpu
from jax.sharding import PartitionSpec as P

SBLK = 16
GRID = 16
LANES = 128
HISTORY = 16
VMEM_LIMIT = 60 * 1024 * 1024


def passed_along(value, axis, steps):
    count = lax.axis_size(axis)
    leading, last = (max(0, -steps), min(count, count - steps))
    return lax.ppermute(value, axis, [(source, source + steps) for source in range(leading, last)])


def block_pairs(block_total):
    pairs = [(p, q) for p in range(block_total) for q in range(p + 1, block_total)]
    return np.array(pairs, dtype=np.int32)


def dft_tables(length, chan_size):
    half = length // 2
    channels = length // 2
    width = channels // chan_size // 2
    positions = np.arange(half, dtype=np.int64)[:, None, None]
    tables = []
    for parity in range(2):
        chans = (
            np.arange(chan_size, dtype=np.int64)[:, None] * 2 * width
            + 2 * np.arange(width, dtype=np.int64)[None, :]
            + parity
        )[None]
        angle = ((positions * chans) % length).astype(np.float64) * (2.0 * math.pi / length)
        table = np.stack([np.cos(angle), -np.sin(angle)], axis=2)
        tables.append(table.reshape(half, 2 * channels // 2).astype(jnp.bfloat16))
    return tables


def filter_kernel(early, *refs):
    if early:
        hist_lo, hist_hi, lo_ref, hi_ref, taps_lo_ref, taps_hi_ref, even_ref, odd_ref, wide = refs
        parts = ((hist_lo, lo_ref), (hist_hi, hi_ref))
    else:
        lo_ref, hi_ref, taps_lo_ref, taps_hi_ref, even_ref, odd_ref, wide = refs
        parts = ((lo_ref,), (hi_ref,))
    frames, stations, cols = even_ref.shape
    tap_count = taps_lo_ref.shape[0]
    for side, sources in enumerate(parts):
        if early:
            wide[side, :HISTORY] = jnp.swapaxes(sources[0][...].astype(jnp.float32), 0, 1)
            whole = jnp.swapaxes(sources[1][...].astype(jnp.float32), 0, 1)
            wide[side, HISTORY:] = whole[:frames]
        else:
            wide[side] = jnp.swapaxes(sources[0][...].astype(jnp.float32), 0, 1)
    span = 4
    rows = 16
    for lane in range(0, cols, LANES):
        lanes = slice(lane, lane + LANES)

        def step(index, carry):
            station = pl.multiple_of((index % (stations // rows)) * rows, rows)
            frame = (index // (stations // rows)) * span
            sums = []
            for side, taps_ref in enumerate((taps_lo_ref, taps_hi_ref)):
                values = [
                    wide[side, frame + HISTORY - (tap_count - 1) + k, pl.ds(station, rows), lanes]
                    for k in range(span + tap_count - 1)
                ]
                accs = [jnp.zeros((rows, LANES), jnp.float32) for _ in range(span)]
                for tap in range(tap_count):
                    weight = taps_ref[tap : tap + 1, lanes]
                    for b in range(span):
                        accs[b] = accs[b] + weight * values[b + tap_count - 1 - tap]
                sums.append(accs)
            for b in range(span):
                even_ref[frame + b, pl.ds(station, rows), lanes] = (
                    sums[0][b] + sums[1][b]
                ).astype(jnp.bfloat16)
                odd_ref[frame + b, pl.ds(station, rows), lanes] = (
                    sums[0][b] - sums[1][b]
                ).astype(jnp.bfloat16)
            return carry

        lax.fori_loop(0, (stations // rows) * (frames // span), step, 0)


def filtered_halves(samples, history, taps):
    stations, all_frames, length = samples.shape
    early = history is not None
    frames = HISTORY if early else all_frames - HISTORY
    tap_count = taps.shape[0]
    half = length // 2
    cols = 256
    steps = half // cols
    lo = lambda j: (0, 0, j)
    hi = lambda j: (0, 0, j + steps)
    out = jax.ShapeDtypeStruct((frames, stations, half), jnp.bfloat16)
    out_spec = pl.BlockSpec((frames, stations, cols), lo)
    operands = [samples, samples, taps, taps]
    specs = [
        pl.BlockSpec((stations, all_frames, cols), lo),
        pl.BlockSpec((stations, all_frames, cols), hi),
        pl.BlockSpec((tap_count, cols), lambda j: (0, j)),
        pl.BlockSpec((tap_count, cols), lambda j: (0, j + steps)),
    ]
    if early:
        operands = [history, history] + operands
        specs = [
            pl.BlockSpec((stations, HISTORY, cols), lo),
            pl.BlockSpec((stations, HISTORY, cols), hi),
        ] + specs
    return pl.pallas_call(
        functools.partial(filter_kernel, early),
        grid=(steps,),
        in_specs=specs,
        out_specs=[out_spec, out_spec],
        out_shape=[out, out],
        scratch_shapes=[pltpu.VMEM((2, HISTORY + frames, stations, cols), jnp.float32)],
        compiler_params=pltpu.CompilerParams(vmem_limit_bytes=VMEM_LIMIT),
        cost_estimate=pl.CostEstimate(
            flops=2 * tap_count * stations * frames * length,
            bytes_accessed=4 * samples.size,
            transcendentals=0,
        ),
    )(*operands)


def dft_kernel(scale, me_ref, rows_ref, table_ref, out_ref):
    out_ref[0] = (
        jnp.dot(rows_ref[...], table_ref[...], preferred_element_type=jnp.float32) * scale
    ).astype(jnp.bfloat16)


def dft(rows, table, chan_size, scale, me):
    row_count, depth = rows.shape
    width = table.shape[1] // chan_size
    return pl.pallas_call(
        functools.partial(dft_kernel, scale),
        grid_spec=pltpu.PrefetchScalarGridSpec(
            num_scalar_prefetch=1,
            grid=(chan_size,),
            in_specs=[
                pl.BlockSpec((row_count, depth), lambda k, me: (0, 0)),
                pl.BlockSpec((depth, width), lambda k, me: (0, me[0] ^ k)),
            ],
            out_specs=pl.BlockSpec((1, row_count, width), lambda k, me: (k, 0, 0)),
        ),
        out_shape=jax.ShapeDtypeStruct((chan_size, row_count, width), jnp.bfloat16),
        compiler_params=pltpu.CompilerParams(vmem_limit_bytes=VMEM_LIMIT),
        cost_estimate=pl.CostEstimate(
            flops=2 * rows.size * table.shape[1],
            bytes_accessed=2 * (rows.size + table.size + row_count * table.shape[1]),
            transcendentals=0,
        ),
    )(me, rows, table)


def exchanged(blocks, shape):
    count = blocks.shape[0]
    pieces = []
    for k in range(count):
        piece = blocks[k].reshape(shape)
        if k:
            piece = lax.ppermute(piece, "chan", [(c, c ^ k) for c in range(count)])
        pieces.append(piece)
    return pieces


def weights_kernel(shift_ref, u_ref, v_ref, out_ref):
    per_step, rows, cells = out_ref.shape
    first = pl.program_id(0) * per_step
    u_of = lax.broadcasted_iota(jnp.int32, (GRID, cells), 1) // GRID
    v_of = lax.broadcasted_iota(jnp.int32, (GRID, cells), 1) % GRID
    grid_row = lax.broadcasted_iota(jnp.int32, (GRID, cells), 0)
    spread_u = (u_of == grid_row).astype(jnp.bfloat16)
    spread_v = (v_of == grid_row).astype(jnp.bfloat16)
    dims = (((0,), (0,)), ((), ()))
    for k in range(per_step):
        shift = shift_ref[first + k]
        for part in range(rows // LANES):
            where = pl.ds(k * rows + part * LANES, LANES)
            u_part = pltpu.roll(u_ref[:, where].astype(jnp.float32), shift, 1).astype(jnp.bfloat16)
            v_part = pltpu.roll(v_ref[:, where].astype(jnp.float32), shift, 1).astype(jnp.bfloat16)
            u_wide = lax.dot_general(u_part, spread_u, dims, preferred_element_type=jnp.float32)
            v_wide = lax.dot_general(v_part, spread_v, dims, preferred_element_type=jnp.float32)
            out_ref[k, part * LANES : (part + 1) * LANES, :] = (u_wide * v_wide).astype(
                jnp.bfloat16
            )


def grid_weights(kern_u, kern_v, shifts):
    rows = SBLK * SBLK
    blocks = kern_u.shape[1] // rows
    per_step = 8
    spec = pl.BlockSpec((GRID, per_step * rows), lambda m, shift: (0, m))
    return pl.pallas_call(
        weights_kernel,
        grid_spec=pltpu.PrefetchScalarGridSpec(
            num_scalar_prefetch=1,
            grid=(blocks // per_step,),
            in_specs=[spec, spec],
            out_specs=pl.BlockSpec((per_step, rows, GRID * GRID), lambda m, shift: (m, 0, 0)),
        ),
        out_shape=jax.ShapeDtypeStruct((blocks, rows, GRID * GRID), jnp.bfloat16),
        compiler_params=pltpu.CompilerParams(vmem_limit_bytes=VMEM_LIMIT),
    )(shifts, kern_u, kern_v)


def correlate_kernel(
    scale, sources, parity, slot_ref, me_ref, *refs
):
    early_refs, late_refs = refs[:sources], refs[sources : 2 * sources]
    weights_hbm, out_ref = refs[2 * sources : 2 * sources + 2]
    staged, spectra, vis, blocks_a, blocks_b, acc, weights_ref, weights_sem = refs[
        2 * sources + 2 :
    ]
    early_frames, source_stations, width = early_refs[0].shape
    late_frames = late_refs[0].shape[0]
    frames = early_frames + late_frames
    stations = sources * source_stations
    group = width // 2
    tiles, rows, cells = out_ref.shape
    block_rows = stations // SBLK
    pieces = LANES // SBLK
    strip = LANES // 2
    strip_blocks = strip // SBLK
    pitch = rows + 1
    unroll = 4

    copy = pltpu.make_async_copy(weights_hbm, weights_ref, weights_sem)
    copy.start()
    acc[...] = jnp.zeros_like(acc)

    def turn(frame, source_refs, lanes, place):
        for k in range(sources):
            start = pl.multiple_of((me_ref[0] ^ k) * source_stations, source_stations)
            staged[pl.ds(start, source_stations), :] = source_refs[k][frame, :, lanes].astype(
                jnp.float32
            )
        flipped = staged[...].T
        for side in range(2):
            spectra[side, pl.ds(place * pitch, width), :] = flipped[
                :, side * LANES : (side + 1) * LANES
            ]

    def turn_early(frame, carry):
        turn(frame, early_refs, slice(None), frame)
        return carry

    def turn_late(frame, carry):
        turn(frame, late_refs, slice(parity * width, (parity + 1) * width), frame + early_frames)
        return carry

    lax.fori_loop(0, early_frames, turn_early, 0)
    lax.fori_loop(0, late_frames, turn_late, 0)

    lane_piece = lax.broadcasted_iota(jnp.int32, (16, LANES), 1) // SBLK
    masks = [(lane_piece & (1 << bit)) != 0 for bit in range(3)]

    for index in range(stations // strip):
        own_side = index * strip // LANES
        offset = index * strip % LANES
        sides = tuple(range(own_side, 2))

        def channels(step, carry):
            for inner in range(unroll):
                channel = step * unroll + inner
                real = [
                    spectra.at[s][pl.ds(channel, frames, stride=pitch), :] for s in range(2)
                ]
                imag = [
                    spectra.at[s][pl.ds(group + channel, frames, stride=pitch), :]
                    for s in range(2)
                ]
                right = jnp.concatenate(
                    [jnp.concatenate([real[s], imag[s]], axis=0) for s in sides], axis=1
                ).astype(jnp.bfloat16)
                own_real = real[own_side][:, offset : offset + strip]
                own_imag = imag[own_side][:, offset : offset + strip]
                left = jnp.concatenate(
                    [
                        jnp.concatenate([own_real, own_imag], axis=1),
                        jnp.concatenate([own_imag, -own_real], axis=1),
                    ],
                    axis=0,
                ).astype(jnp.bfloat16)
                product = lax.dot_general(
                    left, right, (((0,), (0,)), ((), ())), preferred_element_type=jnp.float32
                )
                for part in range(2):
                    for place, side in enumerate(sides):
                        vis.at[side][pl.ds(part * group + channel, strip, stride=pitch), :] = (
                            product[
                                part * strip : (part + 1) * strip,
                                place * LANES : (place + 1) * LANES,
                            ]
                        )
            return carry

        lax.fori_loop(0, group // unroll, channels, 0)
        if index == 0:
            copy.wait()

        def rearrange(step, tile, target):
            side = own_side + step // strip_blocks
            local = step % strip_blocks
            row = pl.multiple_of(tile * 16, 16)
            for upper in range(2):
                turned = []
                for a in range(pieces):
                    start = (local * SBLK + upper * pieces + a) * pitch + row
                    value = vis[side, pl.ds(start, 16), :]
                    if a:
                        value = pltpu.roll(value, a * SBLK, 1)
                    turned.append(value)
                for bit in range(3):
                    turned = [
                        jnp.where(masks[bit], turned[(x + (1 << bit)) % pieces], turned[x])
                        for x in range(pieces)
                    ]
                for piece in range(pieces):
                    target[piece, pl.ds(row, 16), upper * LANES : (upper + 1) * LANES] = turned[
                        -piece % pieces
                    ].astype(jnp.bfloat16)

        steps = strip_blocks * len(sides)
        per_piece = rows // 16 // pieces

        def first(tile, carry):
            rearrange(0, tile, blocks_a)
            return carry

        lax.fori_loop(0, rows // 16, first, 0)

        def pair_step(pair, carry):
            for odd, (current, following) in enumerate(
                ((blocks_a, blocks_b), (blocks_b, blocks_a))
            ):
                step = 2 * pair + odd
                p = index * strip_blocks + step % strip_blocks
                side = own_side + step // strip_blocks
                next_step = jnp.minimum(step + 1, steps - 1)

                def one_piece(piece, inner):
                    q = side * pieces + piece
                    valid = q > p
                    m = jnp.where(valid, p * (2 * block_rows - p - 1) // 2 + q - p - 1, 0)
                    slot = jnp.where(valid, slot_ref[m], tiles)
                    product = jnp.dot(
                        current[piece], weights_ref[m], preferred_element_type=jnp.float32
                    )
                    for tile in range(per_piece):
                        rearrange(next_step, piece * per_piece + tile, following)
                    acc[slot] += product
                    return inner

                lax.fori_loop(0, pieces, one_piece, 0)
            return carry

        lax.fori_loop(0, steps // 2, pair_step, 0)

    for tile in range(tiles):
        out_ref[tile] = acc[tile] * scale


def gridded(early, late, parity, weights, slot_of_block, me, tile_count, total_frames):
    sources = len(early)
    early_frames, source_stations, width = early[0].shape
    frames = early_frames + late[0].shape[0]
    stations = sources * source_stations
    cells = GRID * GRID
    pitch = width + 1
    whole = pl.BlockSpec(memory_space=pltpu.VMEM)
    scalars = pl.BlockSpec(memory_space=pltpu.SMEM)
    block = pltpu.VMEM((LANES // SBLK, width, SBLK * SBLK), jnp.bfloat16)
    return pl.pallas_call(
        functools.partial(correlate_kernel, 1.0 / math.sqrt(total_frames), sources, parity),
        in_specs=[scalars, scalars] + [whole] * (2 * sources) + [pl.BlockSpec(memory_space=pl.ANY)],
        out_specs=whole,
        out_shape=jax.ShapeDtypeStruct((tile_count, width, cells), jnp.float32),
        scratch_shapes=[
            pltpu.VMEM((stations, width), jnp.float32),
            pltpu.VMEM((2, -(-frames * pitch // 8) * 8, LANES), jnp.float32),
            pltpu.VMEM((2, LANES // 2 * pitch, LANES), jnp.float32),
            block,
            block,
            pltpu.VMEM((tile_count + 1, width, cells), jnp.float32),
            pltpu.VMEM(weights.shape, weights.dtype),
            pltpu.SemaphoreType.DMA,
        ],
        compiler_params=pltpu.CompilerParams(vmem_limit_bytes=VMEM_LIMIT),
        cost_estimate=pl.CostEstimate(
            flops=8 * weights.size * width,
            bytes_accessed=2 * weights.size,
            transcendentals=0,
        ),
    )(slot_of_block, me, *early, *late, weights)


def body(samples, taps, block_tile, tile_slots, kern_u, kern_v):
    station_count, frame_count, length = samples.shape
    chan_size = lax.axis_size("chan")
    tm_size = lax.axis_size("tm")
    half = length // 2
    history = passed_along(samples[:, frame_count - HISTORY :], "tm", 1)
    me = lax.axis_index("chan").astype(jnp.int32).reshape(1)
    tables = [jnp.asarray(table) for table in dft_tables(length, chan_size)]
    dft_scale = 1.0 / math.sqrt(length)

    tile_count = tile_slots.shape[0]
    slot_ids = jnp.arange(tile_count, dtype=jnp.int32)
    tile_match = block_tile[:, None] == tile_slots[None, :]
    slot_of_block = jnp.sum(jnp.where(tile_match, slot_ids[None, :], 0), axis=1).astype(jnp.int32)
    pairs = block_pairs(station_count * chan_size // SBLK)
    pieces = LANES // SBLK
    shifts = jnp.asarray((pairs[:, 1] % pieces) * SBLK, jnp.int32)
    weights = grid_weights(kern_u, kern_v, shifts)

    def spectra_of(rows_in, parity):
        rows_in = rows_in.reshape(rows_in.shape[0] * station_count, half)
        return dft(rows_in, tables[parity], chan_size, dft_scale, me)

    late_rows = filtered_halves(samples, None, taps)
    late_blocks = jnp.concatenate([spectra_of(late_rows[0], 0), spectra_of(late_rows[1], 1)], axis=2)
    late = exchanged(late_blocks, (frame_count - HISTORY, station_count, late_blocks.shape[2]))
    early_rows = filtered_halves(samples, history, taps)

    grids = []
    for parity in range(2):
        early_blocks = spectra_of(early_rows[parity], parity)
        early = exchanged(early_blocks, (HISTORY, station_count, early_blocks.shape[2]))
        partial_grid = gridded(
            early, late, parity, weights, slot_of_block, me, tile_count, frame_count * tm_size
        )
        owned = lax.psum_scatter(partial_grid, "tm", scatter_dimension=0, tiled=True)
        owned_tiles, rows, cells = owned.shape
        owned = owned.reshape(owned_tiles, 2, rows // 2, cells).transpose(0, 2, 1, 3)
        grids.append(owned[:, :, None])
    uv_grid = jnp.concatenate(grids, axis=2)
    return uv_grid.reshape(uv_grid.shape[0], -1, 2, uv_grid.shape[-1])


def solution(mesh):
    placed = (P("chan", "tm", None), P(), P(), P(), P(), P())
    return jax.shard_map(
        body, mesh=mesh, in_specs=placed, out_specs=P("tm", "chan", None, None), check_vma=False
    )
```

time: 683 us -> 467 us (0.68)
  Pallas kernels: 457 us -> 269 us
  blocking collectives: 42.3 us -> 0 us
  starting transfers between devices: 10.7 us -> 28.4 us
  waiting for transfers between devices: 150 us -> 137 us
    pallas_call x2, Pallas kernels: 386 us -> 180 us  [gridded(): pl.pallas_call(functools.partial(correlate_kernel, 1.0 / math.sqrt(total_...]
    all_to_all x1 -> x0, blocking collectives: 42.3 us -> none  [body(): lax.all_to_all(spectrum, 'chan', split_axis=0, concat_axis=0, tiled=True)]
    ppermute x0 -> x21, waiting for transfers between devices: none -> 38.5 us  [exchanged(): piece = lax.ppermute(piece, 'chan', [(c, c ^ k) for c in range(count)])]
    ppermute x1, waiting for transfers between devices: 87.9 us -> 52.9 us  [passed_along(): lax.ppermute(value, axis, [(source, source + steps) for source in range(l...]
    ppermute x0 -> x21, starting transfers between devices: none -> 21.3 us  [exchanged(): piece = lax.ppermute(piece, 'chan', [(c, c ^ k) for c in range(count)])]
    all_to_all x1 -> x0, waiting for transfers between devices: 18.8 us -> none  [body(): lax.all_to_all(spectrum, 'chan', split_axis=0, concat_axis=0, tiled=True)]
    pallas_call x3 -> x6, Pallas kernels: 52.4 us -> 70.2 us  [the longest x4 38.6 us: dft(): pl.pallas_call(functools.partial(dft_kernel, scale), grid_spec=pltpu.Pref...]
  transfers between devices with their start and end apart: 4 -> 24, of which waited for: 3 -> 8; matrix products, arithmetic and copies ran while one was open for 0% -> 2% of each run, Pallas kernels for 33% -> 38%
where the time goes in v2:
time: 467 us; the launch traced here: 465 us
  Pallas kernels  269 us (58%)
  waiting for transfers between devices  137 us (29%)
  starting transfers between devices  28.4 us (6%)
  between operations  13.6 us (3%)
  local copies, waits for them, and re-layouts  12.9 us (3%)
    pallas_call x2, Pallas kernels, gridded(): pl.pallas_call(functools.partial(correlate_kernel, 1.0 / math.sqrt(total_...  180 us
    ppermute x1, waiting for transfers between devices, passed_along(): lax.ppermute(value, axis, [(source, source + steps) for source in range(l...  52.9 us
    reduce_scatter x2, waiting for transfers between devices, body(): lax.psum_scatter(partial_grid, 'tm', scatter_dimension=0, tiled=True)  46 us
    pallas_call x4, Pallas kernels, dft(): pl.pallas_call(functools.partial(dft_kernel, scale), grid_spec=pltpu.Pref...  38.6 us
    ppermute x21, waiting for transfers between devices, exchanged(): piece = lax.ppermute(piece, 'chan', [(c, c ^ k) for c in range(count)])  38.5 us
    pallas_call x2, Pallas kernels, filtered_halves(): pl.pallas_call(functools.partial(filter_kernel, early), grid=(steps,), in...  31.7 us
    ppermute x21, starting transfers between devices, exchanged(): piece = lax.ppermute(piece, 'chan', [(c, c ^ k) for c in range(count)])  21.3 us
    pallas_call x1, Pallas kernels, grid_weights(): pl.pallas_call(weights_kernel, grid_spec=pltpu.PrefetchScalarGridSpec(num...  18.5 us
  transfers between devices with their start and end apart: 24, of which 8 were waited for; matrix products, arithmetic and copies ran while one was open for 2% of the time, Pallas kernels for 38%

profile of v2, /device:TPU:0, one launch (start us, length us, event | category | flops | bytes accessed | tf_op | source)
XLA Modules:
  0.0 465.4 jit_solution(1229180686324277222)
XLA Ops:
  6.5 4.7 %slice.75 = bf16[32,16,4096]{2,1,0:T(8,128)(2,1)} slice(bf16[32,24,4096]{2,1,0:T(8,128)(2,1)} %refs_1_.1), slice={[0:32], [8:24], [0:4096]} | slice | bytes 8388608 | tf_op jit(solution)/shard_map/slice | solution.py:414
  11.3 6.9 %collective-permute-start = (bf16[32,16,4096]{2,1,0:T(8,128)(2,1)}, bf16[32,16,4096]{2,1,0:T(8,128)(2,1)}, u32[]{:S(2)}, u32[]{:S(2)}) collective-permute-start(bf16[32,16,4096]{2,1,0:T(8,128)(2,1)} %slice.75), channel_id=1, source_target_pairs={{0,1},{1,2},{2,3},{4,5},{5,6},{6,7},{8,9},{9,10},{10,11},{12,13},{... | collective-permute-start | bytes 12582920 | tf_op jit(solution)/shard_map/ppermute | solution.py:22
  18.1 11.8 %shard_map.93 = (bf16[8,32,2048]{2,1,0:T(8,128)(2,1)}, bf16[8,32,2048]{2,1,0:T(8,128)(2,1)}) custom-call(bf16[32,24,4096]{2,1,0:T(8,128)(2,1)} %refs_1_.1, bf16[32,24,4096]{2,1,0:T(8,128)(2,1)} %refs_1_.1, f32[16,4096]{1,0:T(8,128)} %refs_3_.3, f32[16,4096]{1,0:T(8,128)} %refs_3_.3), custom_call_target="tpu_custom_call" | custom-call | flops 33554432 | bytes 12582912 | tf_op jit(solution)/shard_map/pallas_call | solution.py:121
  30.0 8.7 %shard_map.94 = bf16[8,256,256]{2,1,0:T(8,128)(2,1)} custom-call(s32[1]{0:T(128)} %bitcast.me_ref, bf16[256,2048]{1,0:T(8,128)(2,1)} %bitcast.41, bf16[2048,2048]{1,0:T(8,128)(2,1)} %constant.14.clone.table_ref), custom_call_target="tpu_custom_call" | custom-call | flops 2147483648 | bytes 10485760 | tf_op jit(solution)/shard_map/pallas_call | solution.py:146
  38.6 8.8 %shard_map.95 = bf16[8,256,256]{2,1,0:T(8,128)(2,1)} custom-call(s32[1]{0:T(128)} %bitcast.me_ref, bf16[256,2048]{1,0:T(8,128)(2,1)} %bitcast.40, bf16[2048,2048]{1,0:T(8,128)(2,1)} %constant.15.clone.table_ref), custom_call_target="tpu_custom_call" | custom-call | flops 2147483648 | bytes 10485760 | tf_op jit(solution)/shard_map/pallas_call | solution.py:146
  47.4 2.1 pad_maximum_fusion.1
  53.4 52.9 %collective-permute-done.refs_0_.refs_1_ = bf16[32,16,4096]{2,1,0:T(8,128)(2,1)} collective-permute-done((bf16[32,16,4096]{2,1,0:T(8,128)(2,1)}, bf16[32,16,4096]{2,1,0:T(8,128)(2,1)}, u32[]{:S(2)}, u32[]{:S(2)}) %collective-permute-start) | collective-permute-done | bytes 4194336 | tf_op jit(solution)/shard_map/ppermute | solution.py:22
  107.8 19.9 %shard_map.91 = (bf16[16,32,2048]{2,1,0:T(8,128)(2,1)}, bf16[16,32,2048]{2,1,0:T(8,128)(2,1)}) custom-call(bf16[32,16,4096]{2,1,0:T(8,128)(2,1)} %collective-permute-done.refs_0_.refs_1_, bf16[32,16,4096]{2,1,0:T(8,128)(2,1)} %collective-permute-done.refs_0_.refs_1_, bf16[32,24,4096]{2,1,0:T(8,128)(2,1)} %refs_1_.1, bf16[32,24,4096]{2,1,0:T(8,128)(2,1)} %refs_1_.1, ...), custom_call_target="tpu_custom_call" | custom-call | flops 67108864 | bytes 12582912 | tf_op jit(solution)/shard_map/pallas_call | solution.py:121
  127.7 10.5 %shard_map.92 = bf16[8,512,256]{2,1,0:T(8,128)(2,1)} custom-call(s32[1]{0:T(128)} %bitcast.me_ref, bf16[512,2048]{1,0:T(8,128)(2,1)} %bitcast.70, bf16[2048,2048]{1,0:T(8,128)(2,1)} %constant.14.clone.table_ref), custom_call_target="tpu_custom_call" | custom-call | flops 4294967296 | bytes 12582912 | tf_op jit(solution)/shard_map/pallas_call | solution.py:146
  138.2 2.3 fusion.7
  143.6 2.0 collective-permute-start.7
  146.3 19.7 %collective-permute-done.12.refs_13_ = bf16[8,32,512]{2,1,0:T(8,128)(2,1)S(1)} collective-permute-done((bf16[8,32,512]{2,1,0:T(8,128)(2,1)S(1)}, bf16[8,32,512]{2,1,0:T(8,128)(2,1)S(1)}, u32[]{:S(2)}, u32[]{:S(2)}) %collective-permute-start.12) | collective-permute-done | bytes 262176 | tf_op jit(solution)/shard_map/ppermute | solution.py:173
  168.5 18.5 %shard_map.96.refs_16_ = bf16[120,256,256]{2,1,0:T(8,128)(2,1)} custom-call(s32[120]{0:T(128)} %constant.16.clone.shift_ref, bf16[16,30720]{1,0:T(8,128)(2,1)} %u_ref.1, bf16[16,30720]{1,0:T(8,128)(2,1)} %v_ref.1), custom_call_target="tpu_custom_call" | custom-call | tf_op jit(solution)/shard_map/pallas_call | solution.py:205
  188.5 90.2 %shard_map.97 = f32[8,256,256]{2,1,0:T(8,128)} custom-call(s32[120]{0:T(128)} %select_reduce_fusion.slot_ref, s32[1]{0:T(128)} %bitcast.me_ref, bf16[16,32,256]{2,1,0:T(8,128)(2,1)} %bitcast.46, bf16[16,32,256]{2,1,0:T(8,128)(2,1)} %collective-permute-done.1.refs_1_, bf16[16,32,256]{2,1,0:T(8,128)(2,1)} %collective-permute-done.2.refs_2_, ...), custom_call_target="tpu_custom_call" | custom-call | flops 16106127360 | bytes 15728640 | tf_op jit(solution)/shard_map/pallas_call | solution.py:385
  279.0 10.6 %shard_map.98 = bf16[8,512,256]{2,1,0:T(8,128)(2,1)} custom-call(s32[1]{0:T(128)} %bitcast.me_ref, bf16[512,2048]{1,0:T(8,128)(2,1)} %bitcast.69, bf16[2048,2048]{1,0:T(8,128)(2,1)} %constant.15.clone.table_ref), custom_call_target="tpu_custom_call" | custom-call | flops 4294967296 | bytes 12582912 | tf_op jit(solution)/shard_map/pallas_call | solution.py:146
  289.6 2.3 fusion.8
  292.0 2.6 collective-permute-start.20
  297.6 4.5 collective-permute-done.20.refs_6_
  303.7 3.3 collective-permute-done.21.refs_7_
  307.5 5.1 %collective-permute-done.19.refs_5_ = bf16[16,32,256]{2,1,0:T(8,128)(2,1)S(1)} collective-permute-done((bf16[16,32,256]{2,1,0:T(8,128)(2,1)S(1)}, bf16[16,32,256]{2,1,0:T(8,128)(2,1)S(1)}, u32[]{:S(2)}, u32[]{:S(2)}) %collective-permute-start.19) | collective-permute-done | bytes 262176 | tf_op jit(solution)/shard_map/ppermute | solution.py:173
  312.5 5.7 %collective-permute-done.18.refs_4_ = bf16[16,32,256]{2,1,0:T(8,128)(2,1)S(1)} collective-permute-done((bf16[16,32,256]{2,1,0:T(8,128)(2,1)S(1)}, bf16[16,32,256]{2,1,0:T(8,128)(2,1)S(1)}, u32[]{:S(2)}, u32[]{:S(2)}) %collective-permute-start.18) | collective-permute-done | bytes 262176 | tf_op jit(solution)/shard_map/ppermute | solution.py:173
  319.2 90.2 %shard_map.99 = f32[8,256,256]{2,1,0:T(8,128)} custom-call(s32[120]{0:T(128)} %select_reduce_fusion.slot_ref, s32[1]{0:T(128)} %bitcast.me_ref, bf16[16,32,256]{2,1,0:T(8,128)(2,1)} %bitcast.57, bf16[16,32,256]{2,1,0:T(8,128)(2,1)} %copy-done.17, bf16[16,32,256]{2,1,0:T(8,128)(2,1)} %copy-done.16, bf16[16,32,256]{2,1,0:T(8,128)(2,1)} %copy-done.14, ...), custom_call_target="tpu_custom_call" | custom-call | flops 16106127360 | bytes 15728640 | tf_op jit(solution)/shard_map/pallas_call | solution.py:385
  409.5 46.0 %reduce-scatter.5.cloned.1.call-done = f32[2,256,256]{2,1,0:T(8,128)} async-done(((f32[8,256,256]{2,1,0:T(8,128)}), f32[2,256,256]{2,1,0:T(8,128)}) %reduce-scatter.5.cloned.1.call-update) | async-done | bytes 524304 | tf_op jit(solution)/shard_map/reduce_scatter | solution.py:444
  456.8 1.8 copy.11
  (82 shorter events, 20.7 us)
Async XLA Ops:
  6.5 403.0 %reduce-scatter.3.cloned.1.call-start = ((), (), s32[]{:S(2)}) async-start(), calls=%async_computation.2 | async-start | bytes 2621440 | tf_op jit(solution)/shard_map/reduce_scatter | solution.py:444
  11.3 95.1 %collective-permute-start = (bf16[32,16,4096]{2,1,0:T(8,128)(2,1)}, bf16[32,16,4096]{2,1,0:T(8,128)(2,1)}, u32[]{:S(2)}, u32[]{:S(2)}) collective-permute-start(bf16[32,16,4096]{2,1,0:T(8,128)(2,1)} %slice.75), channel_id=1, source_target_pairs={{0,1},{1,2},{2,3},{4,5},{5,6},{6,7},{8,9},{9,10},{10,11},{12,13},{... | collective-permute-start | bytes 12582920 | tf_op jit(solution)/shard_map/ppermute | solution.py:22
  49.5 91.0 %collective-permute-start.14 = (bf16[8,32,512]{2,1,0:T(8,128)(2,1)S(1)}, bf16[8,32,512]{2,1,0:T(8,128)(2,1)S(1)}, u32[]{:S(2)}, u32[]{:S(2)}) collective-permute-start(bf16[8,32,512]{2,1,0:T(8,128)(2,1)S(1)} %bitcast.63), channel_id=1, source_target_pairs={{0,28},{4,24},{8,20},{12,16},{16,12},{20,8},{24,4},{28,0},{1,29},{... | collective-permute-start | bytes 786440 | tf_op jit(solution)/shard_map/ppermute | solution.py:173
  51.1 89.5 %collective-permute-start.8 = (bf16[8,32,512]{2,1,0:T(8,128)(2,1)S(1)}, bf16[8,32,512]{2,1,0:T(8,128)(2,1)S(1)}, u32[]{:S(2)}, u32[]{:S(2)}) collective-permute-start(bf16[8,32,512]{2,1,0:T(8,128)(2,1)S(1)} %bitcast.60), channel_id=1, source_target_pairs={{0,4},{4,0},{8,12},{12,8},{16,20},{20,16},{24,28},{28,24},{1,5},{5... | collective-permute-start | bytes 786440 | tf_op jit(solution)/shard_map/ppermute | solution.py:173
  52.1 90.1 %collective-permute-start.9 = (bf16[8,32,512]{2,1,0:T(8,128)(2,1)S(1)}, bf16[8,32,512]{2,1,0:T(8,128)(2,1)S(1)}, u32[]{:S(2)}, u32[]{:S(2)}) collective-permute-start(bf16[8,32,512]{2,1,0:T(8,128)(2,1)S(1)} %bitcast.58), channel_id=1, source_target_pairs={{0,8},{4,12},{8,0},{12,4},{16,24},{20,28},{24,16},{28,20},{1,9},{5... | collective-permute-start | bytes 786440 | tf_op jit(solution)/shard_map/ppermute | solution.py:173
  52.6 91.0 %collective-permute-start.10 = (bf16[8,32,512]{2,1,0:T(8,128)(2,1)S(1)}, bf16[8,32,512]{2,1,0:T(8,128)(2,1)}, u32[]{:S(2)}, u32[]{:S(2)}) collective-permute-start(bf16[8,32,512]{2,1,0:T(8,128)(2,1)S(1)} %bitcast.55), channel_id=1, source_target_pairs={{0,12},{4,8},{8,4},{12,0},{16,28},{20,24},{24,20},{28,16},{1,13},{... | collective-permute-start | bytes 786440 | tf_op jit(solution)/shard_map/ppermute | solution.py:173
  106.3 39.4 %collective-permute-start.11 = (bf16[8,32,512]{2,1,0:T(8,128)(2,1)S(1)}, bf16[8,32,512]{2,1,0:T(8,128)(2,1)}, u32[]{:S(2)}, u32[]{:S(2)}) collective-permute-start(bf16[8,32,512]{2,1,0:T(8,128)(2,1)S(1)} %bitcast.54), channel_id=1, source_target_pairs={{0,16},{4,20},{8,24},{12,28},{16,0},{20,4},{24,8},{28,12},{1,17},{... | collective-permute-start | bytes 786440 | tf_op jit(solution)/shard_map/ppermute | solution.py:173
  140.6 25.5 %collective-permute-start.12 = (bf16[8,32,512]{2,1,0:T(8,128)(2,1)S(1)}, bf16[8,32,512]{2,1,0:T(8,128)(2,1)S(1)}, u32[]{:S(2)}, u32[]{:S(2)}) collective-permute-start(bf16[8,32,512]{2,1,0:T(8,128)(2,1)S(1)} %bitcast.51), channel_id=1, source_target_pairs={{0,20},{4,16},{8,28},{12,24},{16,4},{20,0},{24,12},{28,8},{1,21},{... | collective-permute-start | bytes 786440 | tf_op jit(solution)/shard_map/ppermute | solution.py:173
  140.6 25.9 %collective-permute-start.13 = (bf16[8,32,512]{2,1,0:T(8,128)(2,1)S(1)}, bf16[8,32,512]{2,1,0:T(8,128)(2,1)S(1)}, u32[]{:S(2)}, u32[]{:S(2)}) collective-permute-start(bf16[8,32,512]{2,1,0:T(8,128)(2,1)S(1)} %bitcast.48), channel_id=1, source_target_pairs={{0,24},{4,28},{8,16},{12,20},{16,8},{20,12},{24,0},{28,4},{1,25},{... | collective-permute-start | bytes 786440 | tf_op jit(solution)/shard_map/ppermute | solution.py:173
  142.2 25.4 %collective-permute-start.6 = (bf16[16,32,256]{2,1,0:T(8,128)(2,1)S(1)}, bf16[16,32,256]{2,1,0:T(8,128)(2,1)S(1)}, u32[]{:S(2)}, u32[]{:S(2)}) collective-permute-start(bf16[16,32,256]{2,1,0:T(8,128)(2,1)S(1)} %bitcast.59), channel_id=1, source_target_pairs={{0,24},{4,28},{8,16},{12,20},{16,8},{20,12},{24,0},{28,4},{1,25},{... | collective-permute-start | bytes 786440 | tf_op jit(solution)/shard_map/ppermute | solution.py:173
  143.6 24.5 %collective-permute-start.7 = (bf16[16,32,256]{2,1,0:T(8,128)(2,1)S(1)}, bf16[16,32,256]{2,1,0:T(8,128)(2,1)S(1)}, u32[]{:S(2)}, u32[]{:S(2)}) collective-permute-start(bf16[16,32,256]{2,1,0:T(8,128)(2,1)S(1)} %bitcast.56), channel_id=1, source_target_pairs={{0,28},{4,24},{8,20},{12,16},{16,12},{20,8},{24,4},{28,0},{1,29},{... | collective-permute-start | bytes 786440 | tf_op jit(solution)/shard_map/ppermute | solution.py:173
  145.7 41.9 %collective-permute-start.5 = (bf16[16,32,256]{2,1,0:T(8,128)(2,1)S(1)}, bf16[16,32,256]{2,1,0:T(8,128)(2,1)S(1)}, u32[]{:S(2)}, u32[]{:S(2)}) collective-permute-start(bf16[16,32,256]{2,1,0:T(8,128)(2,1)S(1)} %bitcast.53), channel_id=1, source_target_pairs={{0,20},{4,16},{8,28},{12,24},{16,4},{20,0},{24,12},{28,8},{1,21},{... | collective-permute-start | bytes 786440 | tf_op jit(solution)/shard_map/ppermute | solution.py:173
  166.1 21.5 %collective-permute-start.4 = (bf16[16,32,256]{2,1,0:T(8,128)(2,1)S(1)}, bf16[16,32,256]{2,1,0:T(8,128)(2,1)S(1)}, u32[]{:S(2)}, u32[]{:S(2)}) collective-permute-start(bf16[16,32,256]{2,1,0:T(8,128)(2,1)S(1)} %bitcast.52), channel_id=1, source_target_pairs={{0,16},{4,20},{8,24},{12,28},{16,0},{20,4},{24,8},{28,12},{1,17},{... | collective-permute-start | bytes 786440 | tf_op jit(solution)/shard_map/ppermute | solution.py:173
  166.5 21.1 %collective-permute-start.3 = (bf16[16,32,256]{2,1,0:T(8,128)(2,1)S(1)}, bf16[16,32,256]{2,1,0:T(8,128)(2,1)S(1)}, u32[]{:S(2)}, u32[]{:S(2)}) collective-permute-start(bf16[16,32,256]{2,1,0:T(8,128)(2,1)S(1)} %bitcast.50), channel_id=1, source_target_pairs={{0,12},{4,8},{8,4},{12,0},{16,28},{20,24},{24,20},{28,16},{1,13},{... | collective-permute-start | bytes 786440 | tf_op jit(solution)/shard_map/ppermute | solution.py:173
  167.6 20.0 %collective-permute-start.2 = (bf16[16,32,256]{2,1,0:T(8,128)(2,1)S(1)}, bf16[16,32,256]{2,1,0:T(8,128)(2,1)}, u32[]{:S(2)}, u32[]{:S(2)}) collective-permute-start(bf16[16,32,256]{2,1,0:T(8,128)(2,1)S(1)} %bitcast.49), channel_id=1, source_target_pairs={{0,8},{4,12},{8,0},{12,4},{16,24},{20,28},{24,16},{28,20},{1,9},{5... | collective-permute-start | bytes 786440 | tf_op jit(solution)/shard_map/ppermute | solution.py:173
  168.1 19.5 %collective-permute-start.1 = (bf16[16,32,256]{2,1,0:T(8,128)(2,1)S(1)}, bf16[16,32,256]{2,1,0:T(8,128)(2,1)}, u32[]{:S(2)}, u32[]{:S(2)}) collective-permute-start(bf16[16,32,256]{2,1,0:T(8,128)(2,1)S(1)} %bitcast.47), channel_id=1, source_target_pairs={{0,4},{4,0},{8,12},{12,8},{16,20},{20,16},{24,28},{28,24},{1,5},{5... | collective-permute-start | bytes 786440 | tf_op jit(solution)/shard_map/ppermute | solution.py:173
  278.8 176.7 %reduce-scatter.5.cloned.1.call-start = ((), (), s32[]{:S(2)}) async-start(), calls=%async_computation.3 | async-start | bytes 2621440 | tf_op jit(solution)/shard_map/reduce_scatter | solution.py:444
  292.0 10.1 %collective-permute-start.20 = (bf16[16,32,256]{2,1,0:T(8,128)(2,1)S(1)}, bf16[16,32,256]{2,1,0:T(8,128)(2,1)S(1)}, u32[]{:S(2)}, u32[]{:S(2)}) collective-permute-start(bf16[16,32,256]{2,1,0:T(8,128)(2,1)S(1)} %bitcast.68), channel_id=1, source_target_pairs={{0,24},{4,28},{8,16},{12,20},{16,8},{20,12},{24,0},{28,4},{1,25},{... | collective-permute-start | bytes 786440 | tf_op jit(solution)/shard_map/ppermute | solution.py:173
  294.6 12.3 %collective-permute-start.21 = (bf16[16,32,256]{2,1,0:T(8,128)(2,1)S(1)}, bf16[16,32,256]{2,1,0:T(8,128)(2,1)S(1)}, u32[]{:S(2)}, u32[]{:S(2)}) collective-permute-start(bf16[16,32,256]{2,1,0:T(8,128)(2,1)S(1)} %bitcast.67), channel_id=1, source_target_pairs={{0,28},{4,24},{8,20},{12,16},{16,12},{20,8},{24,4},{28,0},{1,29},{... | collective-permute-start | bytes 786440 | tf_op jit(solution)/shard_map/ppermute | solution.py:173
  294.6 17.9 %collective-permute-start.19 = (bf16[16,32,256]{2,1,0:T(8,128)(2,1)S(1)}, bf16[16,32,256]{2,1,0:T(8,128)(2,1)S(1)}, u32[]{:S(2)}, u32[]{:S(2)}) collective-permute-start(bf16[16,32,256]{2,1,0:T(8,128)(2,1)S(1)} %bitcast.66), channel_id=1, source_target_pairs={{0,20},{4,16},{8,28},{12,24},{16,4},{20,0},{24,12},{28,8},{1,21},{... | collective-permute-start | bytes 786440 | tf_op jit(solution)/shard_map/ppermute | solution.py:173
  296.3 21.9 %collective-permute-start.18 = (bf16[16,32,256]{2,1,0:T(8,128)(2,1)S(1)}, bf16[16,32,256]{2,1,0:T(8,128)(2,1)S(1)}, u32[]{:S(2)}, u32[]{:S(2)}) collective-permute-start(bf16[16,32,256]{2,1,0:T(8,128)(2,1)S(1)} %bitcast.65), channel_id=1, source_target_pairs={{0,16},{4,20},{8,24},{12,28},{16,0},{20,4},{24,8},{28,12},{1,17},{... | collective-permute-start | bytes 786440 | tf_op jit(solution)/shard_map/ppermute | solution.py:173
  296.7 21.5 %collective-permute-start.17 = (bf16[16,32,256]{2,1,0:T(8,128)(2,1)S(1)}, bf16[16,32,256]{2,1,0:T(8,128)(2,1)S(1)}, u32[]{:S(2)}, u32[]{:S(2)}) collective-permute-start(bf16[16,32,256]{2,1,0:T(8,128)(2,1)S(1)} %bitcast.64), channel_id=1, source_target_pairs={{0,12},{4,8},{8,4},{12,0},{16,28},{20,24},{24,20},{28,16},{1,13},{... | collective-permute-start | bytes 786440 | tf_op jit(solution)/shard_map/ppermute | solution.py:173
  302.1 16.3 %collective-permute-start.16 = (bf16[16,32,256]{2,1,0:T(8,128)(2,1)S(1)}, bf16[16,32,256]{2,1,0:T(8,128)(2,1)S(1)}, u32[]{:S(2)}, u32[]{:S(2)}) collective-permute-start(bf16[16,32,256]{2,1,0:T(8,128)(2,1)S(1)} %bitcast.62), channel_id=1, source_target_pairs={{0,8},{4,12},{8,0},{12,4},{16,24},{20,28},{24,16},{28,20},{1,9},{5... | collective-permute-start | bytes 786440 | tf_op jit(solution)/shard_map/ppermute | solution.py:173
  307.0 11.5 %collective-permute-start.15 = (bf16[16,32,256]{2,1,0:T(8,128)(2,1)S(1)}, bf16[16,32,256]{2,1,0:T(8,128)(2,1)S(1)}, u32[]{:S(2)}, u32[]{:S(2)}) collective-permute-start(bf16[16,32,256]{2,1,0:T(8,128)(2,1)S(1)} %bitcast.61), channel_id=1, source_target_pairs={{0,4},{4,0},{8,12},{12,8},{16,20},{20,16},{24,28},{28,24},{1,5},{5... | collective-permute-start | bytes 786440 | tf_op jit(solution)/shard_map/ppermute | solution.py:173
  (20 other events, 302.5 us)
Sparse Core Ops, SparseCore 0:
  278.9 46.1 reduce-scatter.2
  409.6 45.8 reduce-scatter.4

commit v3 on v2

--- a/solution.py
+++ b/solution.py
@@ -127,7 +127,7 @@
         scratch_shapes=[pltpu.VMEM((2, HISTORY + frames, stations, cols), jnp.float32)],
         compiler_params=pltpu.CompilerParams(vmem_limit_bytes=VMEM_LIMIT),
         cost_estimate=pl.CostEstimate(
-            flops=2 * tap_count * stations * frames * length,
+            flops=640 * tap_count * stations * frames * length,
             bytes_accessed=4 * samples.size,
             transcendentals=0,
         ),
@@ -212,11 +212,14 @@
         ),
         out_shape=jax.ShapeDtypeStruct((blocks, rows, GRID * GRID), jnp.bfloat16),
         compiler_params=pltpu.CompilerParams(vmem_limit_bytes=VMEM_LIMIT),
+        cost_estimate=pl.CostEstimate(
+            flops=2048 * blocks * rows * GRID, bytes_accessed=0, transcendentals=0
+        ),
     )(shifts, kern_u, kern_v)
 
 
 def correlate_kernel(
-    scale, sources, parity, slot_ref, me_ref, *refs
+    scale, sources, parity, owned, slot_ref, me_ref, owner_ref, *refs
 ):
     early_refs, late_refs = refs[:sources], refs[sources : 2 * sources]
     weights_hbm, out_ref = refs[2 * sources : 2 * sources + 2]
@@ -234,7 +237,9 @@
     strip = LANES // 2
     strip_blocks = strip // SBLK
     pitch = rows + 1
-    unroll = 4
+    unroll = 8
+    span = 4
+    owners = tiles // owned
 
     copy = pltpu.make_async_copy(weights_hbm, weights_ref, weights_sem)
     copy.start()
@@ -341,16 +346,13 @@
 
         lax.fori_loop(0, rows // 16, first, 0)
 
-        def pair_step(pair, carry):
-            for odd, (current, following) in enumerate(
-                ((blocks_a, blocks_b), (blocks_b, blocks_a))
-            ):
-                step = 2 * pair + odd
-                p = index * strip_blocks + step % strip_blocks
-                side = own_side + step // strip_blocks
-                next_step = jnp.minimum(step + 1, steps - 1)
-
-                def one_piece(piece, inner):
+        def pieces_step(step, begin, current, following, gridding):
+            p = index * strip_blocks + step % strip_blocks
+            side = own_side + step // strip_blocks
+            next_step = jnp.minimum(step + 1, steps - 1)
+            for inner in range(span):
+                piece = begin + inner
+                if gridding:
                     q = side * pieces + piece
                     valid = q > p
                     m = jnp.where(valid, p * (2 * block_rows - p - 1) // 2 + q - p - 1, 0)
@@ -358,21 +360,40 @@
                     product = jnp.dot(
                         current[piece], weights_ref[m], preferred_element_type=jnp.float32
                     )
-                    for tile in range(per_piece):
-                        rearrange(next_step, piece * per_piece + tile, following)
+                for tile in range(per_piece):
+                    rearrange(next_step, piece * per_piece + tile, following)
+                if gridding:
                     acc[slot] += product
-                    return inner
-
-                lax.fori_loop(0, pieces, one_piece, 0)
-            return carry
-
-        lax.fori_loop(0, steps // 2, pair_step, 0)
-
-    for tile in range(tiles):
-        out_ref[tile] = acc[tile] * scale
-
-
-def gridded(early, late, parity, weights, slot_of_block, me, tile_count, total_frames):
+
+        for place, side in enumerate(sides):
+            lower = side == own_side and offset >= span * SBLK
+
+            def pair_step(pair, carry):
+                for odd, (current, following) in enumerate(
+                    ((blocks_a, blocks_b), (blocks_b, blocks_a))
+                ):
+                    step = place * strip_blocks + 2 * pair + odd
+
+                    def some_pieces(turn_index, inner):
+                        pieces_step(step, turn_index * span, current, following, True)
+                        return inner
+
+                    if lower:
+                        pieces_step(step, 0, current, following, False)
+                        pieces_step(step, span, current, following, True)
+                    else:
+                        lax.fori_loop(0, pieces // span, some_pieces, 0)
+                return carry
+
+            lax.fori_loop(0, strip_blocks // 2, pair_step, 0)
+
+    for k in range(owners):
+        first_tile = (owner_ref[0] + k) % owners * owned
+        for tile in range(owned):
+            out_ref[k * owned + tile] = (acc[first_tile + tile] * scale).astype(out_ref.dtype)
+
+
+def gridded(early, late, parity, weights, slot_of_block, me, owner, tile_count, total_frames, owned):
     sources = len(early)
     early_frames, source_stations, width = early[0].shape
     frames = early_frames + late[0].shape[0]
@@ -383,10 +404,12 @@
     scalars = pl.BlockSpec(memory_space=pltpu.SMEM)
     block = pltpu.VMEM((LANES // SBLK, width, SBLK * SBLK), jnp.bfloat16)
     return pl.pallas_call(
-        functools.partial(correlate_kernel, 1.0 / math.sqrt(total_frames), sources, parity),
-        in_specs=[scalars, scalars] + [whole] * (2 * sources) + [pl.BlockSpec(memory_space=pl.ANY)],
+        functools.partial(
+            correlate_kernel, 1.0 / math.sqrt(total_frames), sources, parity, owned
+        ),
+        in_specs=[scalars] * 3 + [whole] * (2 * sources) + [pl.BlockSpec(memory_space=pl.ANY)],
         out_specs=whole,
-        out_shape=jax.ShapeDtypeStruct((tile_count, width, cells), jnp.float32),
+        out_shape=jax.ShapeDtypeStruct((tile_count, width, cells), jnp.bfloat16),
         scratch_shapes=[
             pltpu.VMEM((stations, width), jnp.float32),
             pltpu.VMEM((2, -(-frames * pitch // 8) * 8, LANES), jnp.float32),
@@ -399,11 +422,11 @@
         ],
         compiler_params=pltpu.CompilerParams(vmem_limit_bytes=VMEM_LIMIT),
         cost_estimate=pl.CostEstimate(
-            flops=8 * weights.size * width,
+            flops=48 * weights.size * width,
             bytes_accessed=2 * weights.size,
             transcendentals=0,
         ),
-    )(slot_of_block, me, *early, *late, weights)
+    )(slot_of_block, me, owner, *early, *late, weights)
 
 
 def body(samples, taps, block_tile, tile_slots, kern_u, kern_v):
@@ -432,19 +455,40 @@
     late_rows = filtered_halves(samples, None, taps)
     late_blocks = jnp.concatenate([spectra_of(late_rows[0], 0), spectra_of(late_rows[1], 1)], axis=2)
     late = exchanged(late_blocks, (frame_count - HISTORY, station_count, late_blocks.shape[2]))
-    early_rows = filtered_halves(samples, history, taps)
-
+    early_taps, weights = lax.optimization_barrier((taps, weights))
+    early_rows = filtered_halves(samples, history, early_taps)
+    early_blocks = [spectra_of(early_rows[parity], parity) for parity in range(2)]
+    even_weights, early_blocks[1] = lax.optimization_barrier((weights, early_blocks[1]))
+
+    owner = lax.axis_index("tm").astype(jnp.int32).reshape(1)
+    owned = tile_count // tm_size
     grids = []
     for parity in range(2):
-        early_blocks = spectra_of(early_rows[parity], parity)
-        early = exchanged(early_blocks, (HISTORY, station_count, early_blocks.shape[2]))
+        blocks = early_blocks[parity]
+        early = exchanged(blocks, (HISTORY, station_count, blocks.shape[2]))
         partial_grid = gridded(
-            early, late, parity, weights, slot_of_block, me, tile_count, frame_count * tm_size
+            early,
+            late,
+            parity,
+            even_weights if parity == 0 else weights,
+            slot_of_block,
+            me,
+            owner,
+            tile_count,
+            frame_count * tm_size,
+            owned,
         )
-        owned = lax.psum_scatter(partial_grid, "tm", scatter_dimension=0, tiled=True)
-        owned_tiles, rows, cells = owned.shape
-        owned = owned.reshape(owned_tiles, 2, rows // 2, cells).transpose(0, 2, 1, 3)
-        grids.append(owned[:, :, None])
+        total = partial_grid[:owned].astype(jnp.float32)
+        for k in range(1, tm_size):
+            piece = lax.ppermute(
+                partial_grid[k * owned : (k + 1) * owned],
+                "tm",
+                [(z, (z + k) % tm_size) for z in range(tm_size)],
+            )
+            total = total + piece.astype(jnp.float32)
+        _, rows, cells = total.shape
+        total = total.reshape(owned, 2, rows // 2, cells).transpose(0, 2, 1, 3)
+        grids.append(total[:, :, None])
     uv_grid = jnp.concatenate(grids, axis=2)
     return uv_grid.reshape(uv_grid.shape[0], -1, 2, uv_grid.shape[-1])
 

time: 467 us -> 339 us (0.73)
  Pallas kernels: 269 us -> 201 us
  waiting for transfers between devices: 137 us -> 79.2 us
  between operations: 13.6 us -> 0.15 us
  starting transfers between devices: 28.4 us -> 38.6 us
    pallas_call x2, Pallas kernels: 180 us -> 113 us  [gridded(): pl.pallas_call(functools.partial(correlate_kernel, 1.0 / math.sqrt(total_...]
    reduce_scatter x2 -> x0, waiting for transfers between devices: 46 us -> none  [body(): lax.psum_scatter(partial_grid, 'tm', scatter_dimension=0, tiled=True)]
    ppermute x0 -> x6, waiting for transfers between devices: none -> 20.5 us  [body(): lax.ppermute(partial_grid[k * owned:(k + 1) * owned], 'tm', [(z, (z + k)...]
    ppermute x1, waiting for transfers between devices: 52.9 us -> 34.9 us  [passed_along(): lax.ppermute(value, axis, [(source, source + steps) for source in range(l...]
    ppermute x21, waiting for transfers between devices: 38.5 us -> 23.8 us  [exchanged(): piece = lax.ppermute(piece, 'chan', [(c, c ^ k) for c in range(count)])]
    ppermute x0 -> x6, starting transfers between devices: none -> 9.56 us  [body(): lax.ppermute(partial_grid[k * owned:(k + 1) * owned], 'tm', [(z, (z + k)...]
  transfers between devices with their start and end apart: 24 -> 28, of which waited for: 8 -> 10; matrix products, arithmetic and copies ran while one was open for 2% -> 2% of each run, Pallas kernels for 38% -> 60%
where the time goes in v3:
time: 339 us; the launch traced here: 337 us
  Pallas kernels  201 us (59%)
  waiting for transfers between devices  79.2 us (23%)
  starting transfers between devices  38.6 us (11%)
  local copies, waits for them, and re-layouts  12.6 us (4%)
  other arithmetic  5.14 us (2%)
    pallas_call x2, Pallas kernels, gridded(): pl.pallas_call(functools.partial(correlate_kernel, 1.0 / math.sqrt(total_...  113 us
    pallas_call x4, Pallas kernels, dft(): pl.pallas_call(functools.partial(dft_kernel, scale), grid_spec=pltpu.Pref...  38.5 us
    ppermute x1, waiting for transfers between devices, passed_along(): lax.ppermute(value, axis, [(source, source + steps) for source in range(l...  34.9 us
    pallas_call x2, Pallas kernels, filtered_halves(): pl.pallas_call(functools.partial(filter_kernel, early), grid=(steps,), in...  31.7 us
    ppermute x21, waiting for transfers between devices, exchanged(): piece = lax.ppermute(piece, 'chan', [(c, c ^ k) for c in range(count)])  23.8 us
    ppermute x21, starting transfers between devices, exchanged(): piece = lax.ppermute(piece, 'chan', [(c, c ^ k) for c in range(count)])  22.2 us
    ppermute x6, waiting for transfers between devices, body(): lax.ppermute(partial_grid[k * owned:(k + 1) * owned], 'tm', [(z, (z + k)...  20.5 us
    pallas_call x1, Pallas kernels, grid_weights(): pl.pallas_call(weights_kernel, grid_spec=pltpu.PrefetchScalarGridSpec(num...  18.5 us
  transfers between devices with their start and end apart: 28, of which 10 were waited for; matrix products, arithmetic and copies ran while one was open for 2% of the time, Pallas kernels for 60%

profile of v3, /device:TPU:0, one launch (start us, length us, event | category | flops | bytes accessed | tf_op | source)
XLA Modules:
  0.0 337.1 jit_solution(7701894061971489816)
XLA Ops:
  0.0 4.6 %slice.99 = bf16[32,16,4096]{2,1,0:T(8,128)(2,1)} slice(bf16[32,24,4096]{2,1,0:T(8,128)(2,1)} %refs_1_.1), slice={[0:32], [8:24], [0:4096]} | slice | bytes 8388608 | tf_op jit(solution)/shard_map/slice | solution.py:437
  4.6 6.9 %collective-permute-start = (bf16[32,16,4096]{2,1,0:T(8,128)(2,1)}, bf16[32,16,4096]{2,1,0:T(8,128)(2,1)}, u32[]{:S(2)}, u32[]{:S(2)}) collective-permute-start(bf16[32,16,4096]{2,1,0:T(8,128)(2,1)} %slice.99), channel_id=1, source_target_pairs={{0,1},{1,2},{2,3},{4,5},{5,6},{6,7},{8,9},{9,10},{10,11},{12,13},{... | collective-permute-start | bytes 12582920 | tf_op jit(solution)/shard_map/ppermute | solution.py:22
  11.5 11.8 %shard_map.94 = (bf16[8,32,2048]{2,1,0:T(8,128)(2,1)}, bf16[8,32,2048]{2,1,0:T(8,128)(2,1)}) custom-call(bf16[32,24,4096]{2,1,0:T(8,128)(2,1)} %refs_1_.1, bf16[32,24,4096]{2,1,0:T(8,128)(2,1)} %refs_1_.1, f32[16,4096]{1,0:T(8,128)} %refs_3_.3, f32[16,4096]{1,0:T(8,128)} %refs_3_.3), custom_call_target="tpu_custom_call" | custom-call | flops 10737418240 | bytes 12582912 | tf_op jit(solution)/shard_map/pallas_call | solution.py:121
  23.3 8.7 %shard_map.96 = bf16[8,256,256]{2,1,0:T(8,128)(2,1)} custom-call(s32[1]{0:T(128)} %bitcast.me_ref, bf16[256,2048]{1,0:T(8,128)(2,1)} %bitcast.44, bf16[2048,2048]{1,0:T(8,128)(2,1)} %constant.18.clone.table_ref), custom_call_target="tpu_custom_call" | custom-call | flops 2147483648 | bytes 10485760 | tf_op jit(solution)/shard_map/pallas_call | solution.py:146
  32.0 8.8 %shard_map.95 = bf16[8,256,256]{2,1,0:T(8,128)(2,1)} custom-call(s32[1]{0:T(128)} %bitcast.me_ref, bf16[256,2048]{1,0:T(8,128)(2,1)} %bitcast.43, bf16[2048,2048]{1,0:T(8,128)(2,1)} %constant.17.clone.table_ref), custom_call_target="tpu_custom_call" | custom-call | flops 2147483648 | bytes 10485760 | tf_op jit(solution)/shard_map/pallas_call | solution.py:146
  40.7 2.2 pad_maximum_fusion.1
  46.3 18.5 %shard_map.91.refs_16_ = bf16[120,256,256]{2,1,0:T(8,128)(2,1)} custom-call(s32[120]{0:T(128)} %constant.19.clone.shift_ref, bf16[16,30720]{1,0:T(8,128)(2,1)} %u_ref.1, bf16[16,30720]{1,0:T(8,128)(2,1)} %v_ref.1), custom_call_target="tpu_custom_call" | custom-call | flops 1006632960 | tf_op jit(solution)/shard_map/pallas_call | solution.py:205
  64.8 34.9 %collective-permute-done.refs_0_.refs_1_ = bf16[32,16,4096]{2,1,0:T(8,128)(2,1)} collective-permute-done((bf16[32,16,4096]{2,1,0:T(8,128)(2,1)}, bf16[32,16,4096]{2,1,0:T(8,128)(2,1)}, u32[]{:S(2)}, u32[]{:S(2)}) %collective-permute-start) | collective-permute-done | bytes 4194336 | tf_op jit(solution)/shard_map/ppermute | solution.py:22
  99.8 19.9 %shard_map.92 = (bf16[16,32,2048]{2,1,0:T(8,128)(2,1)}, bf16[16,32,2048]{2,1,0:T(8,128)(2,1)}) custom-call(bf16[32,16,4096]{2,1,0:T(8,128)(2,1)} %collective-permute-done.refs_0_.refs_1_, bf16[32,16,4096]{2,1,0:T(8,128)(2,1)} %collective-permute-done.refs_0_.refs_1_, bf16[32,24,4096]{2,1,0:T(8,128)(2,1)} %refs_1_.1, bf16[32,24,4096]{2,1,0:T(8,128)(2,1)} %refs_1_.1, ...), custom_call_target="tpu_custom_call" | custom-call | flops 21474836480 | bytes 12582912 | tf_op jit(solution)/shard_map/pallas_call | solution.py:121
  119.6 10.5 %shard_map.97 = bf16[8,512,256]{2,1,0:T(8,128)(2,1)} custom-call(s32[1]{0:T(128)} %bitcast.me_ref, bf16[512,2048]{1,0:T(8,128)(2,1)} %bitcast.69, bf16[2048,2048]{1,0:T(8,128)(2,1)} %constant.18.clone.table_ref), custom_call_target="tpu_custom_call" | custom-call | flops 4294967296 | bytes 12582912 | tf_op jit(solution)/shard_map/pallas_call | solution.py:146
  130.1 10.6 %shard_map.93 = bf16[8,512,256]{2,1,0:T(8,128)(2,1)} custom-call(s32[1]{0:T(128)} %bitcast.me_ref, bf16[512,2048]{1,0:T(8,128)(2,1)} %bitcast.68, bf16[2048,2048]{1,0:T(8,128)(2,1)} %constant.17.clone.table_ref), custom_call_target="tpu_custom_call" | custom-call | flops 4294967296 | bytes 12582912 | tf_op jit(solution)/shard_map/pallas_call | solution.py:146
  141.4 2.4 collective-permute-start.13
  148.0 3.0 collective-permute-done.13.refs_14_
  153.8 3.9 %collective-permute-done.14.refs_15_ = bf16[8,32,512]{2,1,0:T(8,128)(2,1)S(1)} collective-permute-done((bf16[8,32,512]{2,1,0:T(8,128)(2,1)S(1)}, bf16[8,32,512]{2,1,0:T(8,128)(2,1)S(1)}, u32[]{:S(2)}, u32[]{:S(2)}) %collective-permute-start.14) | collective-permute-done | bytes 262176 | tf_op jit(solution)/shard_map/ppermute | solution.py:173
  159.3 3.3 collective-permute-done.19.refs_2_
  164.6 3.1 collective-permute-done.20.refs_3_
  175.5 4.8 %collective-permute-done.24.refs_7_ = bf16[16,32,256]{2,1,0:T(8,128)(2,1)} collective-permute-done((bf16[16,32,256]{2,1,0:T(8,128)(2,1)S(1)}, bf16[16,32,256]{2,1,0:T(8,128)(2,1)}, u32[]{:S(2)}, u32[]{:S(2)}) %collective-permute-start.24) | collective-permute-done | bytes 262176 | tf_op jit(solution)/shard_map/ppermute | solution.py:173
  182.0 3.3 collective-permute-done.2.refs_2_
  187.1 56.5 %shard_map.99 = bf16[8,256,256]{2,1,0:T(8,128)(2,1)} custom-call(s32[120]{0:T(128)} %select_reduce_fusion.slot_ref, s32[1]{0:T(128)} %bitcast.me_ref, s32[1]{0:T(128)} %bitcast.1.owner_ref, bf16[16,32,256]{2,1,0:T(8,128)(2,1)} %bitcast.48, bf16[16,32,256]{2,1,0:T(8,128)(2,1)} %copy-done.6, bf16[16,32,256]{2,1,0:T(8,128)(2,1)} %copy-done.7, ...), custom_call_target="tpu_custom_call" | custom-call | flops 96636764160 | bytes 15728640 | tf_op jit(solution)/shard_map/pallas_call | solution.py:406
  244.8 4.6 %collective-permute-start.27 = (bf16[2,256,256]{2,1,0:T(8,128)(2,1)S(1)}, bf16[2,256,256]{2,1,0:T(8,128)(2,1)S(1)}, u32[]{:S(2)}, u32[]{:S(2)}) collective-permute-start(bf16[2,256,256]{2,1,0:T(8,128)(2,1)S(1)} %get-tuple-element.49), channel_id=1, source_target_pairs={{0,3},{1,0},{2,1},{3,2},{4,7},{5,4},{6,5},{7,6},{8,11},{9,8},{10,9... | collective-permute-start | bytes 786440 | tf_op jit(solution)/shard_map/ppermute | solution.py:483
  251.2 56.3 %shard_map.98 = bf16[8,256,256]{2,1,0:T(8,128)(2,1)} custom-call(s32[120]{0:T(128)} %select_reduce_fusion.slot_ref, s32[1]{0:T(128)} %bitcast.me_ref, s32[1]{0:T(128)} %bitcast.1.owner_ref, bf16[16,32,256]{2,1,0:T(8,128)(2,1)} %bitcast.47, bf16[16,32,256]{2,1,0:T(8,128)(2,1)} %copy-done.8, bf16[16,32,256]{2,1,0:T(8,128)(2,1)} %collective-permute-done.2.refs_2_, ...), custom_call_target="tpu_custom_call" | custom-call | flops 96636764160 | bytes 15728640 | tf_op jit(solution)/shard_map/pallas_call | solution.py:406
  308.6 2.9 collective-permute-start.17
  313.7 4.7 %collective-permute-done.17 = bf16[2,256,256]{2,1,0:T(8,128)(2,1)S(1)} collective-permute-done((bf16[2,256,256]{2,1,0:T(8,128)(2,1)S(1)}, bf16[2,256,256]{2,1,0:T(8,128)(2,1)S(1)}, u32[]{:S(2)}, u32[]{:S(2)}) %collective-permute-start.17) | collective-permute-done | bytes 262176 | tf_op jit(solution)/shard_map/ppermute | solution.py:483
  318.4 15.8 %collective-permute-done.16 = bf16[2,256,256]{2,1,0:T(8,128)(2,1)S(1)} collective-permute-done((bf16[2,256,256]{2,1,0:T(8,128)(2,1)S(1)}, bf16[2,256,256]{2,1,0:T(8,128)(2,1)S(1)}, u32[]{:S(2)}, u32[]{:S(2)}) %collective-permute-start.16) | collective-permute-done | bytes 262176 | tf_op jit(solution)/shard_map/ppermute | solution.py:483
  (86 shorter events, 35.1 us)
Async XLA Ops:
  4.6 95.1 %collective-permute-start = (bf16[32,16,4096]{2,1,0:T(8,128)(2,1)}, bf16[32,16,4096]{2,1,0:T(8,128)(2,1)}, u32[]{:S(2)}, u32[]{:S(2)}) collective-permute-start(bf16[32,16,4096]{2,1,0:T(8,128)(2,1)} %slice.99), channel_id=1, source_target_pairs={{0,1},{1,2},{2,3},{4,5},{5,6},{6,7},{8,9},{9,10},{10,11},{12,13},{... | collective-permute-start | bytes 12582920 | tf_op jit(solution)/shard_map/ppermute | solution.py:22
  43.0 97.8 %collective-permute-start.8 = (bf16[8,32,512]{2,1,0:T(8,128)(2,1)S(1)}, bf16[8,32,512]{2,1,0:T(8,128)(2,1)S(1)}, u32[]{:S(2)}, u32[]{:S(2)}) collective-permute-start(bf16[8,32,512]{2,1,0:T(8,128)(2,1)S(1)} %bitcast.67), channel_id=1, source_target_pairs={{0,4},{4,0},{8,12},{12,8},{16,20},{20,16},{24,28},{28,24},{1,5},{5... | collective-permute-start | bytes 786440 | tf_op jit(solution)/shard_map/ppermute | solution.py:173
  43.0 101.7 %collective-permute-start.9 = (bf16[8,32,512]{2,1,0:T(8,128)(2,1)}, bf16[8,32,512]{2,1,0:T(8,128)(2,1)}, u32[]{:S(2)}, u32[]{:S(2)}) collective-permute-start(bf16[8,32,512]{2,1,0:T(8,128)(2,1)} %bitcast.15), channel_id=1, source_target_pairs={{0,8},{4,12},{8,0},{12,4},{16,24},{20,28},{24,16},{28,20},{1,9},{5... | collective-permute-start | bytes 786440 | tf_op jit(solution)/shard_map/ppermute | solution.py:173
  44.5 101.6 %collective-permute-start.10 = (bf16[8,32,512]{2,1,0:T(8,128)(2,1)}, bf16[8,32,512]{2,1,0:T(8,128)(2,1)}, u32[]{:S(2)}, u32[]{:S(2)}) collective-permute-start(bf16[8,32,512]{2,1,0:T(8,128)(2,1)} %bitcast.16), channel_id=1, source_target_pairs={{0,12},{4,8},{8,4},{12,0},{16,28},{20,24},{24,20},{28,16},{1,13},{... | collective-permute-start | bytes 786440 | tf_op jit(solution)/shard_map/ppermute | solution.py:173
  44.8 101.3 %collective-permute-start.11 = (bf16[8,32,512]{2,1,0:T(8,128)(2,1)S(1)}, bf16[8,32,512]{2,1,0:T(8,128)(2,1)}, u32[]{:S(2)}, u32[]{:S(2)}) collective-permute-start(bf16[8,32,512]{2,1,0:T(8,128)(2,1)S(1)} %bitcast.64), channel_id=1, source_target_pairs={{0,16},{4,20},{8,24},{12,28},{16,0},{20,4},{24,8},{28,12},{1,17},{... | collective-permute-start | bytes 786440 | tf_op jit(solution)/shard_map/ppermute | solution.py:173
  99.7 48.0 %collective-permute-start.12 = (bf16[8,32,512]{2,1,0:T(8,128)(2,1)S(1)}, bf16[8,32,512]{2,1,0:T(8,128)(2,1)}, u32[]{:S(2)}, u32[]{:S(2)}) collective-permute-start(bf16[8,32,512]{2,1,0:T(8,128)(2,1)S(1)} %bitcast.61), channel_id=1, source_target_pairs={{0,20},{4,16},{8,28},{12,24},{16,4},{20,0},{24,12},{28,8},{1,21},{... | collective-permute-start | bytes 786440 | tf_op jit(solution)/shard_map/ppermute | solution.py:173
  144.7 13.0 %collective-permute-start.14 = (bf16[8,32,512]{2,1,0:T(8,128)(2,1)S(1)}, bf16[8,32,512]{2,1,0:T(8,128)(2,1)S(1)}, u32[]{:S(2)}, u32[]{:S(2)}) collective-permute-start(bf16[8,32,512]{2,1,0:T(8,128)(2,1)S(1)} %bitcast.54), channel_id=1, source_target_pairs={{0,28},{4,24},{8,20},{12,16},{16,12},{20,8},{24,4},{28,0},{1,29},{... | collective-permute-start | bytes 786440 | tf_op jit(solution)/shard_map/ppermute | solution.py:173
  146.1 16.6 %collective-permute-start.19 = (bf16[16,32,256]{2,1,0:T(8,128)(2,1)S(1)}, bf16[16,32,256]{2,1,0:T(8,128)(2,1)S(1)}, u32[]{:S(2)}, u32[]{:S(2)}) collective-permute-start(bf16[16,32,256]{2,1,0:T(8,128)(2,1)S(1)} %bitcast.65), channel_id=1, source_target_pairs={{0,8},{4,12},{8,0},{12,4},{16,24},{20,28},{24,16},{28,20},{1,9},{5... | collective-permute-start | bytes 786440 | tf_op jit(solution)/shard_map/ppermute | solution.py:173
  147.7 20.1 %collective-permute-start.20 = (bf16[16,32,256]{2,1,0:T(8,128)(2,1)S(1)}, bf16[16,32,256]{2,1,0:T(8,128)(2,1)S(1)}, u32[]{:S(2)}, u32[]{:S(2)}) collective-permute-start(bf16[16,32,256]{2,1,0:T(8,128)(2,1)S(1)} %bitcast.62), channel_id=1, source_target_pairs={{0,12},{4,8},{8,4},{12,0},{16,28},{20,24},{24,20},{28,16},{1,13},{... | collective-permute-start | bytes 786440 | tf_op jit(solution)/shard_map/ppermute | solution.py:173
  151.0 17.5 %collective-permute-start.21 = (bf16[16,32,256]{2,1,0:T(8,128)(2,1)S(1)}, bf16[16,32,256]{2,1,0:T(8,128)(2,1)S(1)}, u32[]{:S(2)}, u32[]{:S(2)}) collective-permute-start(bf16[16,32,256]{2,1,0:T(8,128)(2,1)S(1)} %bitcast.59), channel_id=1, source_target_pairs={{0,16},{4,20},{8,24},{12,28},{16,0},{20,4},{24,8},{28,12},{1,17},{... | collective-permute-start | bytes 786440 | tf_op jit(solution)/shard_map/ppermute | solution.py:173
  157.7 13.7 %collective-permute-start.22 = (bf16[16,32,256]{2,1,0:T(8,128)(2,1)S(1)}, bf16[16,32,256]{2,1,0:T(8,128)(2,1)}, u32[]{:S(2)}, u32[]{:S(2)}) collective-permute-start(bf16[16,32,256]{2,1,0:T(8,128)(2,1)S(1)} %bitcast.57), channel_id=1, source_target_pairs={{0,20},{4,16},{8,28},{12,24},{16,4},{20,0},{24,12},{28,8},{1,21},{... | collective-permute-start | bytes 786440 | tf_op jit(solution)/shard_map/ppermute | solution.py:173
  158.0 15.7 %collective-permute-start.23 = (bf16[16,32,256]{2,1,0:T(8,128)(2,1)S(1)}, bf16[16,32,256]{2,1,0:T(8,128)(2,1)}, u32[]{:S(2)}, u32[]{:S(2)}) collective-permute-start(bf16[16,32,256]{2,1,0:T(8,128)(2,1)S(1)} %bitcast.55), channel_id=1, source_target_pairs={{0,24},{4,28},{8,16},{12,20},{16,8},{20,12},{24,0},{28,4},{1,25},{... | collective-permute-start | bytes 786440 | tf_op jit(solution)/shard_map/ppermute | solution.py:173
  162.7 17.6 %collective-permute-start.24 = (bf16[16,32,256]{2,1,0:T(8,128)(2,1)S(1)}, bf16[16,32,256]{2,1,0:T(8,128)(2,1)}, u32[]{:S(2)}, u32[]{:S(2)}) collective-permute-start(bf16[16,32,256]{2,1,0:T(8,128)(2,1)S(1)} %bitcast.52), channel_id=1, source_target_pairs={{0,28},{4,24},{8,20},{12,16},{16,12},{20,8},{24,4},{28,0},{1,29},{... | collective-permute-start | bytes 786440 | tf_op jit(solution)/shard_map/ppermute | solution.py:173
  169.2 16.1 %collective-permute-start.2 = (bf16[16,32,256]{2,1,0:T(8,128)(2,1)S(1)}, bf16[16,32,256]{2,1,0:T(8,128)(2,1)}, u32[]{:S(2)}, u32[]{:S(2)}) collective-permute-start(bf16[16,32,256]{2,1,0:T(8,128)(2,1)S(1)} %bitcast.60), channel_id=1, source_target_pairs={{0,8},{4,12},{8,0},{12,4},{16,24},{20,28},{24,16},{28,20},{1,9},{5... | collective-permute-start | bytes 786440 | tf_op jit(solution)/shard_map/ppermute | solution.py:173
  171.4 73.4 %collective-permute-start.3 = (bf16[16,32,256]{2,1,0:T(8,128)(2,1)S(1)}, bf16[16,32,256]{2,1,0:T(8,128)(2,1)S(1)}, u32[]{:S(2)}, u32[]{:S(2)}) collective-permute-start(bf16[16,32,256]{2,1,0:T(8,128)(2,1)S(1)} %bitcast.56), channel_id=1, source_target_pairs={{0,12},{4,8},{8,4},{12,0},{16,28},{20,24},{24,20},{28,16},{1,13},{... | collective-permute-start | bytes 786440 | tf_op jit(solution)/shard_map/ppermute | solution.py:173
  173.6 75.7 %collective-permute-start.4 = (bf16[16,32,256]{2,1,0:T(8,128)(2,1)S(1)}, bf16[16,32,256]{2,1,0:T(8,128)(2,1)S(1)}, u32[]{:S(2)}, u32[]{:S(2)}) collective-permute-start(bf16[16,32,256]{2,1,0:T(8,128)(2,1)S(1)} %bitcast.53), channel_id=1, source_target_pairs={{0,16},{4,20},{8,24},{12,28},{16,0},{20,4},{24,8},{28,12},{1,17},{... | collective-permute-start | bytes 786440 | tf_op jit(solution)/shard_map/ppermute | solution.py:173
  180.3 69.1 %collective-permute-start.5 = (bf16[16,32,256]{2,1,0:T(8,128)(2,1)S(1)}, bf16[16,32,256]{2,1,0:T(8,128)(2,1)}, u32[]{:S(2)}, u32[]{:S(2)}) collective-permute-start(bf16[16,32,256]{2,1,0:T(8,128)(2,1)S(1)} %bitcast.51), channel_id=1, source_target_pairs={{0,20},{4,16},{8,28},{12,24},{16,4},{20,0},{24,12},{28,8},{1,21},{... | collective-permute-start | bytes 786440 | tf_op jit(solution)/shard_map/ppermute | solution.py:173
  180.6 69.8 %collective-permute-start.6 = (bf16[16,32,256]{2,1,0:T(8,128)(2,1)S(1)}, bf16[16,32,256]{2,1,0:T(8,128)(2,1)S(1)}, u32[]{:S(2)}, u32[]{:S(2)}) collective-permute-start(bf16[16,32,256]{2,1,0:T(8,128)(2,1)S(1)} %bitcast.50), channel_id=1, source_target_pairs={{0,24},{4,28},{8,16},{12,20},{16,8},{20,12},{24,0},{28,4},{1,25},{... | collective-permute-start | bytes 786440 | tf_op jit(solution)/shard_map/ppermute | solution.py:173
  185.3 65.1 %collective-permute-start.7 = (bf16[16,32,256]{2,1,0:T(8,128)(2,1)S(1)}, bf16[16,32,256]{2,1,0:T(8,128)(2,1)S(1)}, u32[]{:S(2)}, u32[]{:S(2)}) collective-permute-start(bf16[16,32,256]{2,1,0:T(8,128)(2,1)S(1)} %bitcast.49), channel_id=1, source_target_pairs={{0,28},{4,24},{8,20},{12,16},{16,12},{20,8},{24,4},{28,0},{1,29},{... | collective-permute-start | bytes 786440 | tf_op jit(solution)/shard_map/ppermute | solution.py:173
  244.8 67.8 %collective-permute-start.27 = (bf16[2,256,256]{2,1,0:T(8,128)(2,1)S(1)}, bf16[2,256,256]{2,1,0:T(8,128)(2,1)S(1)}, u32[]{:S(2)}, u32[]{:S(2)}) collective-permute-start(bf16[2,256,256]{2,1,0:T(8,128)(2,1)S(1)} %get-tuple-element.49), channel_id=1, source_target_pairs={{0,3},{1,0},{2,1},{3,2},{4,7},{5,4},{6,5},{7,6},{8,11},{9,8},{10,9... | collective-permute-start | bytes 786440 | tf_op jit(solution)/shard_map/ppermute | solution.py:483
  249.4 63.3 %collective-permute-start.26 = (bf16[2,256,256]{2,1,0:T(8,128)(2,1)S(1)}, bf16[2,256,256]{2,1,0:T(8,128)(2,1)S(1)}, u32[]{:S(2)}, u32[]{:S(2)}) collective-permute-start(bf16[2,256,256]{2,1,0:T(8,128)(2,1)S(1)} %get-tuple-element.50), channel_id=1, source_target_pairs={{0,2},{1,3},{2,0},{3,1},{4,6},{5,7},{6,4},{7,5},{8,10},{9,11},{10,... | collective-permute-start | bytes 786440 | tf_op jit(solution)/shard_map/ppermute | solution.py:483
  249.4 63.3 %collective-permute-start.25 = (bf16[2,256,256]{2,1,0:T(8,128)(2,1)S(1)}, bf16[2,256,256]{2,1,0:T(8,128)(2,1)S(1)}, u32[]{:S(2)}, u32[]{:S(2)}) collective-permute-start(bf16[2,256,256]{2,1,0:T(8,128)(2,1)S(1)} %get-tuple-element.48), channel_id=1, source_target_pairs={{0,1},{1,2},{2,3},{3,0},{4,5},{5,6},{6,7},{7,4},{8,9},{9,10},{10,1... | collective-permute-start | bytes 786440 | tf_op jit(solution)/shard_map/ppermute | solution.py:483
  311.6 22.6 %collective-permute-start.16 = (bf16[2,256,256]{2,1,0:T(8,128)(2,1)S(1)}, bf16[2,256,256]{2,1,0:T(8,128)(2,1)S(1)}, u32[]{:S(2)}, u32[]{:S(2)}) collective-permute-start(bf16[2,256,256]{2,1,0:T(8,128)(2,1)S(1)} %get-tuple-element.47), channel_id=1, source_target_pairs={{0,2},{1,3},{2,0},{3,1},{4,6},{5,7},{6,4},{7,5},{8,10},{9,11},{10,... | collective-permute-start | bytes 786440 | tf_op jit(solution)/shard_map/ppermute | solution.py:483
  312.6 21.6 %collective-permute-start.15 = (bf16[2,256,256]{2,1,0:T(8,128)(2,1)S(1)}, bf16[2,256,256]{2,1,0:T(8,128)(2,1)S(1)}, u32[]{:S(2)}, u32[]{:S(2)}) collective-permute-start(bf16[2,256,256]{2,1,0:T(8,128)(2,1)S(1)} %get-tuple-element.45), channel_id=1, source_target_pairs={{0,1},{1,2},{2,3},{3,0},{4,5},{5,6},{6,7},{7,4},{8,9},{9,10},{10,1... | collective-permute-start | bytes 786440 | tf_op jit(solution)/shard_map/ppermute | solution.py:483
  (21 other events, 182.8 us)

commit v4 on v3

--- a/solution.py
+++ b/solution.py
@@ -41,8 +41,9 @@
         )[None]
         angle = ((positions * chans) % length).astype(np.float64) * (2.0 * math.pi / length)
         table = np.stack([np.cos(angle), -np.sin(angle)], axis=2)
-        tables.append(table.reshape(half, 2 * channels // 2).astype(jnp.bfloat16))
-    return tables
+        table = table.reshape(half, chan_size, 2 * width).transpose(1, 0, 2)
+        tables.append(table.astype(jnp.bfloat16))
+    return np.stack(tables)
 
 
 def filter_kernel(early, *refs):
@@ -93,8 +94,9 @@
         lax.fori_loop(0, (stations // rows) * (frames // span), step, 0)
 
 
-def filtered_halves(samples, history, taps):
+def filtered_halves(samples, history, taps, part=0, parts=1):
     stations, all_frames, length = samples.shape
+    stations = stations // parts
     early = history is not None
     frames = HISTORY if early else all_frames - HISTORY
     tap_count = taps.shape[0]
@@ -107,8 +109,8 @@
     out_spec = pl.BlockSpec((frames, stations, cols), lo)
     operands = [samples, samples, taps, taps]
     specs = [
-        pl.BlockSpec((stations, all_frames, cols), lo),
-        pl.BlockSpec((stations, all_frames, cols), hi),
+        pl.BlockSpec((stations, all_frames, cols), lambda j: (part, 0, j)),
+        pl.BlockSpec((stations, all_frames, cols), lambda j: (part, 0, j + steps)),
         pl.BlockSpec((tap_count, cols), lambda j: (0, j)),
         pl.BlockSpec((tap_count, cols), lambda j: (0, j + steps)),
     ]
@@ -134,34 +136,40 @@
     )(*operands)
 
 
-def dft_kernel(scale, me_ref, rows_ref, table_ref, out_ref):
-    out_ref[0] = (
-        jnp.dot(rows_ref[...], table_ref[...], preferred_element_type=jnp.float32) * scale
-    ).astype(jnp.bfloat16)
-
-
-def dft(rows, table, chan_size, scale, me):
-    row_count, depth = rows.shape
-    width = table.shape[1] // chan_size
+def dft_kernel(scale, me_ref, even_ref, odd_ref, table_ref, out_ref):
+    for parity, rows_ref in enumerate((even_ref, odd_ref)):
+
+        @pl.when(pl.program_id(1) == parity)
+        def _():
+            out_ref[0] = (
+                jnp.dot(rows_ref[...], table_ref[0, 0], preferred_element_type=jnp.float32) * scale
+            ).astype(jnp.bfloat16)
+
+
+def dft(even, odd, tables, scale, me):
+    row_count, depth = even.shape
+    _, chan_size, _, width = tables.shape
+    rows = pl.BlockSpec((row_count, depth), lambda k, parity, me: (0, 0))
     return pl.pallas_call(
         functools.partial(dft_kernel, scale),
         grid_spec=pltpu.PrefetchScalarGridSpec(
             num_scalar_prefetch=1,
-            grid=(chan_size,),
+            grid=(chan_size, 2),
             in_specs=[
-                pl.BlockSpec((row_count, depth), lambda k, me: (0, 0)),
-                pl.BlockSpec((depth, width), lambda k, me: (0, me[0] ^ k)),
+                rows,
+                rows,
+                pl.BlockSpec((1, 1, depth, width), lambda k, parity, me: (parity, me[0] ^ k, 0, 0)),
             ],
-            out_specs=pl.BlockSpec((1, row_count, width), lambda k, me: (k, 0, 0)),
-        ),
-        out_shape=jax.ShapeDtypeStruct((chan_size, row_count, width), jnp.bfloat16),
+            out_specs=pl.BlockSpec((1, row_count, width), lambda k, parity, me: (k, 0, parity)),
+        ),
+        out_shape=jax.ShapeDtypeStruct((chan_size, row_count, 2 * width), jnp.bfloat16),
         compiler_params=pltpu.CompilerParams(vmem_limit_bytes=VMEM_LIMIT),
         cost_estimate=pl.CostEstimate(
-            flops=2 * rows.size * table.shape[1],
-            bytes_accessed=2 * (rows.size + table.size + row_count * table.shape[1]),
+            flops=2 * row_count * tables.size,
+            bytes_accessed=2 * (2 * even.size + tables.size + row_count * 2 * chan_size * width),
             transcendentals=0,
         ),
-    )(me, rows, table)
+    )(me, even, odd, tables)
 
 
 def exchanged(blocks, shape):
@@ -219,15 +227,17 @@
 
 
 def correlate_kernel(
-    scale, sources, parity, owned, slot_ref, me_ref, owner_ref, *refs
+    scale, sources, parts, parity, owned, slot_ref, me_ref, owner_ref, *refs
 ):
-    early_refs, late_refs = refs[:sources], refs[sources : 2 * sources]
-    weights_hbm, out_ref = refs[2 * sources : 2 * sources + 2]
-    staged, spectra, vis, blocks_a, blocks_b, acc, weights_ref, weights_sem = refs[
-        2 * sources + 2 :
-    ]
-    early_frames, source_stations, width = early_refs[0].shape
-    late_frames = late_refs[0].shape[0]
+    early_count = parts * sources
+    early_refs, late_refs = refs[:early_count], refs[early_count : early_count + sources]
+    refs = refs[early_count + sources :]
+    weights_hbm, out_ref = refs[:2]
+    staged, spectra, vis, blocks_a, blocks_b, acc, weights_ref, weights_sem = refs[2:]
+    early_frames = early_refs[0].shape[0]
+    late_frames, source_stations, both = late_refs[0].shape
+    width = both // 2
+    lanes = slice(parity * width, (parity + 1) * width)
     frames = early_frames + late_frames
     stations = sources * source_stations
     group = width // 2
@@ -245,12 +255,15 @@
     copy.start()
     acc[...] = jnp.zeros_like(acc)
 
-    def turn(frame, source_refs, lanes, place):
-        for k in range(sources):
-            start = pl.multiple_of((me_ref[0] ^ k) * source_stations, source_stations)
-            staged[pl.ds(start, source_stations), :] = source_refs[k][frame, :, lanes].astype(
-                jnp.float32
-            )
+    def turn(frame, source_refs, place):
+        count = len(source_refs) // sources
+        rows_each = source_stations // count
+        for part in range(count):
+            for k in range(sources):
+                start = (me_ref[0] ^ k) * source_stations + part * rows_each
+                staged[pl.ds(pl.multiple_of(start, rows_each), rows_each), :] = source_refs[
+                    part * sources + k
+                ][frame, :, lanes].astype(jnp.float32)
         flipped = staged[...].T
         for side in range(2):
             spectra[side, pl.ds(place * pitch, width), :] = flipped[
@@ -258,11 +271,11 @@
             ]
 
     def turn_early(frame, carry):
-        turn(frame, early_refs, slice(None), frame)
+        turn(frame, early_refs, frame)
         return carry
 
     def turn_late(frame, carry):
-        turn(frame, late_refs, slice(parity * width, (parity + 1) * width), frame + early_frames)
+        turn(frame, late_refs, frame + early_frames)
         return carry
 
     lax.fori_loop(0, early_frames, turn_early, 0)
@@ -394,9 +407,11 @@
 
 
 def gridded(early, late, parity, weights, slot_of_block, me, owner, tile_count, total_frames, owned):
-    sources = len(early)
-    early_frames, source_stations, width = early[0].shape
-    frames = early_frames + late[0].shape[0]
+    sources = len(late)
+    parts = len(early) // sources
+    late_frames, source_stations, both = late[0].shape
+    width = both // 2
+    frames = early[0].shape[0] + late_frames
     stations = sources * source_stations
     cells = GRID * GRID
     pitch = width + 1
@@ -405,9 +420,9 @@
     block = pltpu.VMEM((LANES // SBLK, width, SBLK * SBLK), jnp.bfloat16)
     return pl.pallas_call(
         functools.partial(
-            correlate_kernel, 1.0 / math.sqrt(total_frames), sources, parity, owned
-        ),
-        in_specs=[scalars] * 3 + [whole] * (2 * sources) + [pl.BlockSpec(memory_space=pl.ANY)],
+            correlate_kernel, 1.0 / math.sqrt(total_frames), sources, parts, parity, owned
+        ),
+        in_specs=[scalars] * 3 + [whole] * (len(early) + sources) + [pl.BlockSpec(memory_space=pl.ANY)],
         out_specs=whole,
         out_shape=jax.ShapeDtypeStruct((tile_count, width, cells), jnp.bfloat16),
         scratch_shapes=[
@@ -434,9 +449,16 @@
     chan_size = lax.axis_size("chan")
     tm_size = lax.axis_size("tm")
     half = length // 2
-    history = passed_along(samples[:, frame_count - HISTORY :], "tm", 1)
+    parts = 2 if station_count % 32 == 0 else 1
+    part_stations = station_count // parts
+    histories = []
+    for part in range(parts):
+        tail = samples[part * part_stations : (part + 1) * part_stations, frame_count - HISTORY :]
+        if part:
+            tail, histories[-1] = lax.optimization_barrier((tail, histories[-1]))
+        histories.append(passed_along(tail, "tm", 1))
     me = lax.axis_index("chan").astype(jnp.int32).reshape(1)
-    tables = [jnp.asarray(table) for table in dft_tables(length, chan_size)]
+    tables = jnp.asarray(dft_tables(length, chan_size))
     dft_scale = 1.0 / math.sqrt(length)
 
     tile_count = tile_slots.shape[0]
@@ -448,29 +470,31 @@
     shifts = jnp.asarray((pairs[:, 1] % pieces) * SBLK, jnp.int32)
     weights = grid_weights(kern_u, kern_v, shifts)
 
-    def spectra_of(rows_in, parity):
-        rows_in = rows_in.reshape(rows_in.shape[0] * station_count, half)
-        return dft(rows_in, tables[parity], chan_size, dft_scale, me)
-
-    late_rows = filtered_halves(samples, None, taps)
-    late_blocks = jnp.concatenate([spectra_of(late_rows[0], 0), spectra_of(late_rows[1], 1)], axis=2)
-    late = exchanged(late_blocks, (frame_count - HISTORY, station_count, late_blocks.shape[2]))
-    early_taps, weights = lax.optimization_barrier((taps, weights))
-    early_rows = filtered_halves(samples, history, early_taps)
-    early_blocks = [spectra_of(early_rows[parity], parity) for parity in range(2)]
-    even_weights, early_blocks[1] = lax.optimization_barrier((weights, early_blocks[1]))
+    def exchanged_spectra(rows):
+        frames, stations, _ = rows[0].shape
+        even, odd = (half_rows.reshape(frames * stations, half) for half_rows in rows)
+        blocks = dft(even, odd, tables, dft_scale, me)
+        return exchanged(blocks, (frames, stations, blocks.shape[2]))
+
+    late = exchanged_spectra(filtered_halves(samples, None, taps))
+    early_taps = taps
+    early = []
+    for part in range(parts):
+        if part == parts - 1:
+            early_taps, weights = lax.optimization_barrier((taps, weights))
+        early += exchanged_spectra(
+            filtered_halves(samples, histories[part], early_taps, part, parts)
+        )
 
     owner = lax.axis_index("tm").astype(jnp.int32).reshape(1)
     owned = tile_count // tm_size
     grids = []
     for parity in range(2):
-        blocks = early_blocks[parity]
-        early = exchanged(blocks, (HISTORY, station_count, blocks.shape[2]))
         partial_grid = gridded(
             early,
             late,
             parity,
-            even_weights if parity == 0 else weights,
+            weights,
             slot_of_block,
             me,
             owner,

time: 339 us -> 362 us (1.068)
  Pallas kernels: 201 us -> 215 us
  starting transfers between devices: 38.6 us -> 44.2 us
  local copies, waits for them, and re-layouts: 12.6 us -> 17.3 us
    pallas_call x4 -> x3, Pallas kernels: 38.5 us -> 48.8 us  [dft(): pl.pallas_call(functools.partial(dft_kernel, scale), grid_spec=pltpu.Pref...]
    slice x2 -> x3, local copies, waits for them, and re-layouts: 1.73 us -> 7.73 us  [exchanged(): piece = blocks[k].reshape(shape)]
    ppermute x1 -> x2, starting transfers between devices: 6.88 us -> 12 us  [passed_along(): lax.ppermute(value, axis, [(source, source + steps) for source in range(l...]
    ppermute x21, waiting for transfers between devices: 23.8 us -> 28.3 us  [exchanged(): piece = lax.ppermute(piece, 'chan', [(c, c ^ k) for c in range(count)])]
    ppermute x1 -> x2, waiting for transfers between devices: 34.9 us -> 32.1 us  [passed_along(): lax.ppermute(value, axis, [(source, source + steps) for source in range(l...]
    pallas_call x2 -> x3, Pallas kernels: 31.7 us -> 33.4 us  [filtered_halves(): pl.pallas_call(functools.partial(filter_kernel, early), grid=(steps,), in...]
  transfers between devices with their start and end apart: 28 -> 29, of which waited for: 10 -> 12; matrix products, arithmetic and copies ran while one was open for 2% -> 3% of each run, Pallas kernels for 60% -> 44%
where the time goes in v4:
time: 362 us; the launch traced here: 360 us
  Pallas kernels  215 us (59%)
  waiting for transfers between devices  80.6 us (22%)
  starting transfers between devices  44.2 us (12%)
  local copies, waits for them, and re-layouts  17.3 us (5%)
    pallas_call x2, Pallas kernels, gridded(): pl.pallas_call(functools.partial(correlate_kernel, 1.0 / math.sqrt(total_...  114 us
    pallas_call x3, Pallas kernels, dft(): pl.pallas_call(functools.partial(dft_kernel, scale), grid_spec=pltpu.Pref...  48.8 us
    pallas_call x3, Pallas kernels, filtered_halves(): pl.pallas_call(functools.partial(filter_kernel, early), grid=(steps,), in...  33.4 us
    ppermute x2, waiting for transfers between devices, passed_along(): lax.ppermute(value, axis, [(source, source + steps) for source in range(l...  32.1 us
    ppermute x21, waiting for transfers between devices, exchanged(): piece = lax.ppermute(piece, 'chan', [(c, c ^ k) for c in range(count)])  28.3 us
    ppermute x21, starting transfers between devices, exchanged(): piece = lax.ppermute(piece, 'chan', [(c, c ^ k) for c in range(count)])  23.3 us
    ppermute x6, waiting for transfers between devices, body(): lax.ppermute(partial_grid[k * owned:(k + 1) * owned], 'tm', [(z, (z + k)...  20.3 us
    pallas_call x1, Pallas kernels, grid_weights(): pl.pallas_call(weights_kernel, grid_spec=pltpu.PrefetchScalarGridSpec(num...  18.4 us
  transfers between devices with their start and end apart: 29, of which 12 were waited for; matrix products, arithmetic and copies ran while one was open for 3% of the time, Pallas kernels for 44%

profile of v4, /device:TPU:0, one launch (start us, length us, event | category | flops | bytes accessed | tf_op | source)
XLA Modules:
  0.0 359.8 jit_solution(5138551654635133625)
XLA Ops:
  0.0 4.0 %fusion = (bf16[16,16,4096]{2,1,0:T(8,128)(2,1)}, bf16[16,16,4096]{2,1,0:T(8,128)(2,1)S(1)}) fusion(bf16[32,24,4096]{2,1,0:T(8,128)(2,1)} %refs_1_.1), kind=kLoop, calls=%fused_computation.4 | loop fusion | bytes 8388608 | tf_op jit(solution)/shard_map/slice | solution.py:456
  4.0 6.2 %collective-permute-start = (bf16[16,16,4096]{2,1,0:T(8,128)(2,1)}, bf16[16,16,4096]{2,1,0:T(8,128)(2,1)}, u32[]{:S(2)}, u32[]{:S(2)}) collective-permute-start(bf16[16,16,4096]{2,1,0:T(8,128)(2,1)} %get-tuple-element.25), channel_id=1, source_target_pairs={{0,1},{1,2},{2,3},{4,5},{5,6},{6,7},{8,9},{9,10},{10,11},{12,13},{... | collective-permute-start | bytes 6291464 | tf_op jit(solution)/shard_map/ppermute | solution.py:22
  10.2 11.8 %shard_map.87 = (bf16[8,32,2048]{2,1,0:T(8,128)(2,1)}, bf16[8,32,2048]{2,1,0:T(8,128)(2,1)}) custom-call(bf16[32,24,4096]{2,1,0:T(8,128)(2,1)} %refs_1_.1, bf16[32,24,4096]{2,1,0:T(8,128)(2,1)} %refs_1_.1, f32[16,4096]{1,0:T(8,128)} %refs_3_.5, f32[16,4096]{1,0:T(8,128)} %refs_3_.5), custom_call_target="tpu_custom_call" | custom-call | flops 10737418240 | bytes 12582912 | tf_op jit(solution)/shard_map/pallas_call | solution.py:123
  22.0 32.1 %collective-permute-done.refs_0_.refs_1_ = bf16[16,16,4096]{2,1,0:T(8,128)(2,1)} collective-permute-done((bf16[16,16,4096]{2,1,0:T(8,128)(2,1)}, bf16[16,16,4096]{2,1,0:T(8,128)(2,1)}, u32[]{:S(2)}, u32[]{:S(2)}) %collective-permute-start) | collective-permute-done | bytes 2097184 | tf_op jit(solution)/shard_map/ppermute | solution.py:22
  54.1 5.7 %collective-permute-start.8 = (bf16[16,16,4096]{2,1,0:T(8,128)(2,1)S(1)}, bf16[16,16,4096]{2,1,0:T(8,128)(2,1)}, u32[]{:S(2)}, u32[]{:S(2)}) collective-permute-start(bf16[16,16,4096]{2,1,0:T(8,128)(2,1)S(1)} %get-tuple-element.18), channel_id=1, source_target_pairs={{0,1},{1,2},{2,3},{4,5},{5,6},{6,7},{8,9},{9,10},{10,11},{12,13},{... | collective-permute-start | bytes 6291464 | tf_op jit(solution)/shard_map/ppermute | solution.py:22
  59.8 16.2 %shard_map.88 = bf16[8,256,512]{2,1,0:T(8,128)(2,1)} custom-call(s32[1]{0:T(128)} %bitcast.me_ref, bf16[256,2048]{1,0:T(8,128)(2,1)} %bitcast.47, bf16[256,2048]{1,0:T(8,128)(2,1)} %bitcast.48, bf16[2,8,2048,256]{3,2,1,0:T(8,128)(2,1)} %constant.15.clone.table_ref), custom_call_target="tpu_custom_call" | custom-call | flops 4294967296 | bytes 20971520 | tf_op jit(solution)/shard_map/pallas_call | solution.py:153
  83.5 18.4 %shard_map.84.refs_24_ = bf16[120,256,256]{2,1,0:T(8,128)(2,1)} custom-call(s32[120]{0:T(128)} %constant.16.clone.shift_ref, bf16[16,30720]{1,0:T(8,128)(2,1)} %u_ref.1, bf16[16,30720]{1,0:T(8,128)(2,1)} %v_ref.1), custom_call_target="tpu_custom_call" | custom-call | flops 1006632960 | tf_op jit(solution)/shard_map/pallas_call | solution.py:213
  101.9 10.8 %shard_map.82 = (bf16[16,16,2048]{2,1,0:T(8,128)(2,1)}, bf16[16,16,2048]{2,1,0:T(8,128)(2,1)}) custom-call(bf16[16,16,4096]{2,1,0:T(8,128)(2,1)} %collective-permute-done.refs_0_.refs_1_, bf16[16,16,4096]{2,1,0:T(8,128)(2,1)} %collective-permute-done.refs_0_.refs_1_, bf16[32,24,4096]{2,1,0:T(8,128)(2,1)} %refs_1_.1, bf16[32,24,4096]{2,1,0:T(8,128)(2,1)} %refs_1_.1, ...), custom_call_target="tpu_custom_call" | custom-call | flops 10737418240 | bytes 12582912 | tf_op jit(solution)/shard_map/pallas_call | solution.py:123
  112.7 16.3 %shard_map.83 = bf16[8,256,512]{2,1,0:T(8,128)(2,1)} custom-call(s32[1]{0:T(128)} %bitcast.me_ref, bf16[256,2048]{1,0:T(8,128)(2,1)} %bitcast.49, bf16[256,2048]{1,0:T(8,128)(2,1)} %bitcast.50, bf16[2,8,2048,256]{3,2,1,0:T(8,128)(2,1)} %constant.15.clone.table_ref), custom_call_target="tpu_custom_call" | custom-call | flops 4294967296 | bytes 20971520 | tf_op jit(solution)/shard_map/pallas_call | solution.py:153
  132.3 10.8 %shard_map.85 = (bf16[16,16,2048]{2,1,0:T(8,128)(2,1)}, bf16[16,16,2048]{2,1,0:T(8,128)(2,1)}) custom-call(bf16[16,16,4096]{2,1,0:T(8,128)(2,1)} %collective-permute-done.8.refs_0_.refs_1_, bf16[16,16,4096]{2,1,0:T(8,128)(2,1)} %collective-permute-done.8.refs_0_.refs_1_, bf16[32,24,4096]{2,1,0:T(8,128)(2,1)} %refs_1_.1, bf16[32,24,4096]{2,1,0:T(8,128)(2,1)} %refs_1_.1, ...), custom_call_target="tpu_custom_call" | custom-call | flops 10737418240 | bytes 12582912 | tf_op jit(solution)/shard_map/pallas_call | solution.py:123
  143.9 16.3 %shard_map.86 = bf16[8,256,512]{2,1,0:T(8,128)(2,1)} custom-call(s32[1]{0:T(128)} %bitcast.me_ref, bf16[256,2048]{1,0:T(8,128)(2,1)} %bitcast.45, bf16[256,2048]{1,0:T(8,128)(2,1)} %bitcast.46, bf16[2,8,2048,256]{3,2,1,0:T(8,128)(2,1)} %constant.15.clone.table_ref), custom_call_target="tpu_custom_call" | custom-call | flops 4294967296 | bytes 20971520 | tf_op jit(solution)/shard_map/pallas_call | solution.py:153
  172.3 3.2 collective-permute-done.7.refs_7_
  176.1 4.9 %collective-permute-done.5.refs_5_ = bf16[16,16,512]{2,1,0:T(8,128)(2,1)S(1)} collective-permute-done((bf16[16,16,512]{2,1,0:T(8,128)(2,1)S(1)}, bf16[16,16,512]{2,1,0:T(8,128)(2,1)S(1)}, u32[]{:S(2)}, u32[]{:S(2)}) %collective-permute-start.5) | collective-permute-done | bytes 262176 | tf_op jit(solution)/shard_map/ppermute | solution.py:181
  183.4 4.1 %collective-permute-done.4.refs_4_ = bf16[16,16,512]{2,1,0:T(8,128)(2,1)S(1)} collective-permute-done((bf16[16,16,512]{2,1,0:T(8,128)(2,1)S(1)}, bf16[16,16,512]{2,1,0:T(8,128)(2,1)S(1)}, u32[]{:S(2)}, u32[]{:S(2)}) %collective-permute-start.4) | collective-permute-done | bytes 262176 | tf_op jit(solution)/shard_map/ppermute | solution.py:181
  194.8 3.2 collective-permute-done.15.refs_15_
  199.4 4.2 %collective-permute-done.13.refs_13_ = bf16[16,16,512]{2,1,0:T(8,128)(2,1)S(1)} collective-permute-done((bf16[16,16,512]{2,1,0:T(8,128)(2,1)S(1)}, bf16[16,16,512]{2,1,0:T(8,128)(2,1)S(1)}, u32[]{:S(2)}, u32[]{:S(2)}) %collective-permute-start.13) | collective-permute-done | bytes 262176 | tf_op jit(solution)/shard_map/ppermute | solution.py:181
  203.6 5.8 %collective-permute-done.12.refs_12_ = bf16[16,16,512]{2,1,0:T(8,128)(2,1)} collective-permute-done((bf16[16,16,512]{2,1,0:T(8,128)(2,1)S(1)}, bf16[16,16,512]{2,1,0:T(8,128)(2,1)}, u32[]{:S(2)}, u32[]{:S(2)}) %collective-permute-start.12) | collective-permute-done | bytes 262176 | tf_op jit(solution)/shard_map/ppermute | solution.py:181
  210.2 57.2 %shard_map.89 = bf16[8,256,256]{2,1,0:T(8,128)(2,1)} custom-call(s32[120]{0:T(128)} %select_reduce_fusion.slot_ref, s32[1]{0:T(128)} %bitcast.me_ref, s32[1]{0:T(128)} %bitcast.1.owner_ref, bf16[16,16,512]{2,1,0:T(8,128)(2,1)} %bitcast.53, bf16[16,16,512]{2,1,0:T(8,128)(2,1)} %copy-done.11, bf16[16,16,512]{2,1,0:T(8,128)(2,1)} %copy-done.10, ...), custom_call_target="tpu_custom_call" | custom-call | flops 96636764160 | bytes 15728640 | tf_op jit(solution)/shard_map/pallas_call | solution.py:421
  268.8 3.5 collective-permute-start.25
  272.4 57.0 %shard_map.90 = bf16[8,256,256]{2,1,0:T(8,128)(2,1)} custom-call(s32[120]{0:T(128)} %select_reduce_fusion.slot_ref, s32[1]{0:T(128)} %bitcast.me_ref, s32[1]{0:T(128)} %bitcast.1.owner_ref, bf16[16,16,512]{2,1,0:T(8,128)(2,1)} %bitcast.54, bf16[16,16,512]{2,1,0:T(8,128)(2,1)} %copy-done.11, bf16[16,16,512]{2,1,0:T(8,128)(2,1)} %copy-done.10, ...), custom_call_target="tpu_custom_call" | custom-call | flops 96636764160 | bytes 15728640 | tf_op jit(solution)/shard_map/pallas_call | solution.py:421
  331.1 3.3 collective-permute-start.28
  336.6 5.0 %collective-permute-done.26 = bf16[2,256,256]{2,1,0:T(8,128)(2,1)S(1)} collective-permute-done((bf16[2,256,256]{2,1,0:T(8,128)(2,1)S(1)}, bf16[2,256,256]{2,1,0:T(8,128)(2,1)S(1)}, u32[]{:S(2)}, u32[]{:S(2)}) %collective-permute-start.26) | collective-permute-done | bytes 262176 | tf_op jit(solution)/shard_map/ppermute | solution.py:507
  341.7 3.4 collective-permute-done.28
  345.0 11.8 %collective-permute-done.27 = bf16[2,256,256]{2,1,0:T(8,128)(2,1)S(1)} collective-permute-done((bf16[2,256,256]{2,1,0:T(8,128)(2,1)S(1)}, bf16[2,256,256]{2,1,0:T(8,128)(2,1)S(1)}, u32[]{:S(2)}, u32[]{:S(2)}) %collective-permute-start.27) | collective-permute-done | bytes 262176 | tf_op jit(solution)/shard_map/ppermute | solution.py:507
  (92 shorter events, 44.6 us)
Async XLA Ops:
  4.0 50.1 %collective-permute-start = (bf16[16,16,4096]{2,1,0:T(8,128)(2,1)}, bf16[16,16,4096]{2,1,0:T(8,128)(2,1)}, u32[]{:S(2)}, u32[]{:S(2)}) collective-permute-start(bf16[16,16,4096]{2,1,0:T(8,128)(2,1)} %get-tuple-element.25), channel_id=1, source_target_pairs={{0,1},{1,2},{2,3},{4,5},{5,6},{6,7},{8,9},{9,10},{10,11},{12,13},{... | collective-permute-start | bytes 6291464 | tf_op jit(solution)/shard_map/ppermute | solution.py:22
  54.1 77.4 %collective-permute-start.8 = (bf16[16,16,4096]{2,1,0:T(8,128)(2,1)S(1)}, bf16[16,16,4096]{2,1,0:T(8,128)(2,1)}, u32[]{:S(2)}, u32[]{:S(2)}) collective-permute-start(bf16[16,16,4096]{2,1,0:T(8,128)(2,1)S(1)} %get-tuple-element.18), channel_id=1, source_target_pairs={{0,1},{1,2},{2,3},{4,5},{5,6},{6,7},{8,9},{9,10},{10,11},{12,13},{... | collective-permute-start | bytes 6291464 | tf_op jit(solution)/shard_map/ppermute | solution.py:22
  78.8 64.3 %collective-permute-start.21 = (bf16[8,32,512]{2,1,0:T(8,128)(2,1)}, bf16[8,32,512]{2,1,0:T(8,128)(2,1)}, u32[]{:S(2)}, u32[]{:S(2)}) collective-permute-start(bf16[8,32,512]{2,1,0:T(8,128)(2,1)} %bitcast.30), channel_id=1, source_target_pairs={{0,24},{4,28},{8,16},{12,20},{16,8},{20,12},{24,0},{28,4},{1,25},{... | collective-permute-start | bytes 786440 | tf_op jit(solution)/shard_map/ppermute | solution.py:181
  81.2 79.0 %collective-permute-start.22 = (bf16[8,32,512]{2,1,0:T(8,128)(2,1)}, bf16[8,32,512]{2,1,0:T(8,128)(2,1)}, u32[]{:S(2)}, u32[]{:S(2)}) collective-permute-start(bf16[8,32,512]{2,1,0:T(8,128)(2,1)} %bitcast.31), channel_id=1, source_target_pairs={{0,28},{4,24},{8,20},{12,16},{16,12},{20,8},{24,4},{28,0},{1,29},{... | collective-permute-start | bytes 786440 | tf_op jit(solution)/shard_map/ppermute | solution.py:181
  81.3 79.3 %collective-permute-start.20 = (bf16[8,32,512]{2,1,0:T(8,128)(2,1)}, bf16[8,32,512]{2,1,0:T(8,128)(2,1)}, u32[]{:S(2)}, u32[]{:S(2)}) collective-permute-start(bf16[8,32,512]{2,1,0:T(8,128)(2,1)} %bitcast.29), channel_id=1, source_target_pairs={{0,20},{4,16},{8,28},{12,24},{16,4},{20,0},{24,12},{28,8},{1,21},{... | collective-permute-start | bytes 786440 | tf_op jit(solution)/shard_map/ppermute | solution.py:181
  83.0 80.1 %collective-permute-start.19 = (bf16[8,32,512]{2,1,0:T(8,128)(2,1)}, bf16[8,32,512]{2,1,0:T(8,128)(2,1)}, u32[]{:S(2)}, u32[]{:S(2)}) collective-permute-start(bf16[8,32,512]{2,1,0:T(8,128)(2,1)} %bitcast.28), channel_id=1, source_target_pairs={{0,16},{4,20},{8,24},{12,28},{16,0},{20,4},{24,8},{28,12},{1,17},{... | collective-permute-start | bytes 786440 | tf_op jit(solution)/shard_map/ppermute | solution.py:181
  131.5 31.6 %collective-permute-start.18 = (bf16[8,32,512]{2,1,0:T(8,128)(2,1)}, bf16[8,32,512]{2,1,0:T(8,128)(2,1)S(1)}, u32[]{:S(2)}, u32[]{:S(2)}) collective-permute-start(bf16[8,32,512]{2,1,0:T(8,128)(2,1)} %bitcast.27), channel_id=1, source_target_pairs={{0,12},{4,8},{8,4},{12,0},{16,28},{20,24},{24,20},{28,16},{1,13},{... | collective-permute-start | bytes 786440 | tf_op jit(solution)/shard_map/ppermute | solution.py:181
  143.1 21.7 %collective-permute-start.17 = (bf16[8,32,512]{2,1,0:T(8,128)(2,1)S(1)}, bf16[8,32,512]{2,1,0:T(8,128)(2,1)S(1)}, u32[]{:S(2)}, u32[]{:S(2)}) collective-permute-start(bf16[8,32,512]{2,1,0:T(8,128)(2,1)S(1)} %bitcast.67), channel_id=1, source_target_pairs={{0,8},{4,12},{8,0},{12,4},{16,24},{20,28},{24,16},{28,20},{1,9},{5... | collective-permute-start | bytes 786440 | tf_op jit(solution)/shard_map/ppermute | solution.py:181
  163.1 12.3 %collective-permute-start.7 = (bf16[16,16,512]{2,1,0:T(8,128)(2,1)S(1)}, bf16[16,16,512]{2,1,0:T(8,128)(2,1)S(1)}, u32[]{:S(2)}, u32[]{:S(2)}) collective-permute-start(bf16[16,16,512]{2,1,0:T(8,128)(2,1)S(1)} %bitcast.65), channel_id=1, source_target_pairs={{0,28},{4,24},{8,20},{12,16},{16,12},{20,8},{24,4},{28,0},{1,29},{... | collective-permute-start | bytes 786440 | tf_op jit(solution)/shard_map/ppermute | solution.py:181
  163.1 18.0 %collective-permute-start.5 = (bf16[16,16,512]{2,1,0:T(8,128)(2,1)S(1)}, bf16[16,16,512]{2,1,0:T(8,128)(2,1)S(1)}, u32[]{:S(2)}, u32[]{:S(2)}) collective-permute-start(bf16[16,16,512]{2,1,0:T(8,128)(2,1)S(1)} %bitcast.62), channel_id=1, source_target_pairs={{0,20},{4,16},{8,28},{12,24},{16,4},{20,0},{24,12},{28,8},{1,21},{... | collective-permute-start | bytes 786440 | tf_op jit(solution)/shard_map/ppermute | solution.py:181
  165.5 22.0 %collective-permute-start.4 = (bf16[16,16,512]{2,1,0:T(8,128)(2,1)S(1)}, bf16[16,16,512]{2,1,0:T(8,128)(2,1)S(1)}, u32[]{:S(2)}, u32[]{:S(2)}) collective-permute-start(bf16[16,16,512]{2,1,0:T(8,128)(2,1)S(1)} %bitcast.61), channel_id=1, source_target_pairs={{0,16},{4,20},{8,24},{12,28},{16,0},{20,4},{24,8},{28,12},{1,17},{... | collective-permute-start | bytes 786440 | tf_op jit(solution)/shard_map/ppermute | solution.py:181
  168.4 21.0 %collective-permute-start.3 = (bf16[16,16,512]{2,1,0:T(8,128)(2,1)S(1)}, bf16[16,16,512]{2,1,0:T(8,128)(2,1)S(1)}, u32[]{:S(2)}, u32[]{:S(2)}) collective-permute-start(bf16[16,16,512]{2,1,0:T(8,128)(2,1)S(1)} %bitcast.59), channel_id=1, source_target_pairs={{0,12},{4,8},{8,4},{12,0},{16,28},{20,24},{24,20},{28,16},{1,13},{... | collective-permute-start | bytes 786440 | tf_op jit(solution)/shard_map/ppermute | solution.py:181
  170.7 19.4 %collective-permute-start.2 = (bf16[16,16,512]{2,1,0:T(8,128)(2,1)S(1)}, bf16[16,16,512]{2,1,0:T(8,128)(2,1)S(1)}, u32[]{:S(2)}, u32[]{:S(2)}) collective-permute-start(bf16[16,16,512]{2,1,0:T(8,128)(2,1)S(1)} %bitcast.58), channel_id=1, source_target_pairs={{0,8},{4,12},{8,0},{12,4},{16,24},{20,28},{24,16},{28,20},{1,9},{5... | collective-permute-start | bytes 786440 | tf_op jit(solution)/shard_map/ppermute | solution.py:181
  175.4 16.3 %collective-permute-start.1 = (bf16[16,16,512]{2,1,0:T(8,128)(2,1)S(1)}, bf16[16,16,512]{2,1,0:T(8,128)(2,1)S(1)}, u32[]{:S(2)}, u32[]{:S(2)}) collective-permute-start(bf16[16,16,512]{2,1,0:T(8,128)(2,1)S(1)} %bitcast.57), channel_id=1, source_target_pairs={{0,4},{4,0},{8,12},{12,8},{16,20},{20,16},{24,28},{28,24},{1,5},{5... | collective-permute-start | bytes 786440 | tf_op jit(solution)/shard_map/ppermute | solution.py:181
  181.1 12.2 %collective-permute-start.14 = (bf16[16,16,512]{2,1,0:T(8,128)(2,1)S(1)}, bf16[16,16,512]{2,1,0:T(8,128)(2,1)S(1)}, u32[]{:S(2)}, u32[]{:S(2)}) collective-permute-start(bf16[16,16,512]{2,1,0:T(8,128)(2,1)S(1)} %bitcast.72), channel_id=1, source_target_pairs={{0,24},{4,28},{8,16},{12,20},{16,8},{20,12},{24,0},{28,4},{1,25},{... | collective-permute-start | bytes 786440 | tf_op jit(solution)/shard_map/ppermute | solution.py:181
  189.5 14.1 %collective-permute-start.13 = (bf16[16,16,512]{2,1,0:T(8,128)(2,1)S(1)}, bf16[16,16,512]{2,1,0:T(8,128)(2,1)S(1)}, u32[]{:S(2)}, u32[]{:S(2)}) collective-permute-start(bf16[16,16,512]{2,1,0:T(8,128)(2,1)S(1)} %bitcast.69), channel_id=1, source_target_pairs={{0,20},{4,16},{8,28},{12,24},{16,4},{20,0},{24,12},{28,8},{1,21},{... | collective-permute-start | bytes 786440 | tf_op jit(solution)/shard_map/ppermute | solution.py:181
  190.2 19.2 %collective-permute-start.12 = (bf16[16,16,512]{2,1,0:T(8,128)(2,1)S(1)}, bf16[16,16,512]{2,1,0:T(8,128)(2,1)}, u32[]{:S(2)}, u32[]{:S(2)}) collective-permute-start(bf16[16,16,512]{2,1,0:T(8,128)(2,1)S(1)} %bitcast.68), channel_id=1, source_target_pairs={{0,16},{4,20},{8,24},{12,28},{16,0},{20,4},{24,8},{28,12},{1,17},{... | collective-permute-start | bytes 786440 | tf_op jit(solution)/shard_map/ppermute | solution.py:181
  191.7 17.6 %collective-permute-start.11 = (bf16[16,16,512]{2,1,0:T(8,128)(2,1)S(1)}, bf16[16,16,512]{2,1,0:T(8,128)(2,1)}, u32[]{:S(2)}, u32[]{:S(2)}) collective-permute-start(bf16[16,16,512]{2,1,0:T(8,128)(2,1)S(1)} %bitcast.66), channel_id=1, source_target_pairs={{0,12},{4,8},{8,4},{12,0},{16,28},{20,24},{24,20},{28,16},{1,13},{... | collective-permute-start | bytes 786440 | tf_op jit(solution)/shard_map/ppermute | solution.py:181
  193.2 16.1 %collective-permute-start.10 = (bf16[16,16,512]{2,1,0:T(8,128)(2,1)S(1)}, bf16[16,16,512]{2,1,0:T(8,128)(2,1)S(1)}, u32[]{:S(2)}, u32[]{:S(2)}) collective-permute-start(bf16[16,16,512]{2,1,0:T(8,128)(2,1)S(1)} %bitcast.64), channel_id=1, source_target_pairs={{0,8},{4,12},{8,0},{12,4},{16,24},{20,28},{24,16},{28,20},{1,9},{5... | collective-permute-start | bytes 786440 | tf_op jit(solution)/shard_map/ppermute | solution.py:181
  268.5 65.9 %collective-permute-start.23 = (bf16[2,256,256]{2,1,0:T(8,128)(2,1)S(1)}, bf16[2,256,256]{2,1,0:T(8,128)(2,1)S(1)}, u32[]{:S(2)}, u32[]{:S(2)}) collective-permute-start(bf16[2,256,256]{2,1,0:T(8,128)(2,1)S(1)} %get-tuple-element.51), channel_id=1, source_target_pairs={{0,1},{1,2},{2,3},{3,0},{4,5},{5,6},{6,7},{7,4},{8,9},{9,10},{10,1... | collective-permute-start | bytes 786440 | tf_op jit(solution)/shard_map/ppermute | solution.py:507
  268.8 66.7 %collective-permute-start.25 = (bf16[2,256,256]{2,1,0:T(8,128)(2,1)S(1)}, bf16[2,256,256]{2,1,0:T(8,128)(2,1)S(1)}, u32[]{:S(2)}, u32[]{:S(2)}) collective-permute-start(bf16[2,256,256]{2,1,0:T(8,128)(2,1)S(1)} %get-tuple-element.52), channel_id=1, source_target_pairs={{0,3},{1,0},{2,1},{3,2},{4,7},{5,4},{6,5},{7,6},{8,11},{9,8},{10,9... | collective-permute-start | bytes 786440 | tf_op jit(solution)/shard_map/ppermute | solution.py:507
  272.4 63.1 %collective-permute-start.24 = (bf16[2,256,256]{2,1,0:T(8,128)(2,1)S(1)}, bf16[2,256,256]{2,1,0:T(8,128)(2,1)S(1)}, u32[]{:S(2)}, u32[]{:S(2)}) collective-permute-start(bf16[2,256,256]{2,1,0:T(8,128)(2,1)S(1)} %get-tuple-element.53), channel_id=1, source_target_pairs={{0,2},{1,3},{2,0},{3,1},{4,6},{5,7},{6,4},{7,5},{8,10},{9,11},{10,... | collective-permute-start | bytes 786440 | tf_op jit(solution)/shard_map/ppermute | solution.py:507
  331.1 13.9 %collective-permute-start.28 = (bf16[2,256,256]{2,1,0:T(8,128)(2,1)S(1)}, bf16[2,256,256]{2,1,0:T(8,128)(2,1)S(1)}, u32[]{:S(2)}, u32[]{:S(2)}) collective-permute-start(bf16[2,256,256]{2,1,0:T(8,128)(2,1)S(1)} %get-tuple-element.55), channel_id=1, source_target_pairs={{0,3},{1,0},{2,1},{3,2},{4,7},{5,4},{6,5},{7,6},{8,11},{9,8},{10,9... | collective-permute-start | bytes 786440 | tf_op jit(solution)/shard_map/ppermute | solution.py:507
  334.4 22.5 %collective-permute-start.27 = (bf16[2,256,256]{2,1,0:T(8,128)(2,1)S(1)}, bf16[2,256,256]{2,1,0:T(8,128)(2,1)S(1)}, u32[]{:S(2)}, u32[]{:S(2)}) collective-permute-start(bf16[2,256,256]{2,1,0:T(8,128)(2,1)S(1)} %get-tuple-element.56), channel_id=1, source_target_pairs={{0,2},{1,3},{2,0},{3,1},{4,6},{5,7},{6,4},{7,5},{8,10},{9,11},{10,... | collective-permute-start | bytes 786440 | tf_op jit(solution)/shard_map/ppermute | solution.py:507
  (24 other events, 347.1 us)
